TPU v7x, 32 devices: a whole 2x2x4 slice. The times are simulated.
32 devices in a mesh: band: 2 (over x), spk: 16 (over z, y, core).
Axes of the slice: x: 2, y: 2, z: 4, core: 2. Of those that a mesh axis runs over, the one named last changes fastest.
Arguments:
- direction: float32 [64, 128, 128], P(('band', 'spk')), parts along dimension 0, may hold values from -6 to 6
- plant: bfloat16 [832, 2, 128, 128], P(('band', 'spk')), parts along dimension 0
- tile_pairs: int32 [832, 2], P(('band', 'spk')), parts along dimension 0, may hold values from 0 to 127, as said below
- mic_weight: float32 [2, 128, 128], P('band', 'spk'), parts along dimension 0, may hold values from 0.3 to 3
Outputs:
- hessian_vector: float32 [64, 128, 128], P(('band', 'spk')), parts along dimension 0
There are 2 independent parts, one for each index of `band`. A program takes and returns all parts, laid end to end along the dimension named above; each array names one. Nothing has to cross between parts.
Inputs may be any that keep to these rules, and one draw needn't show every extreme that they name: `tile_pairs`: column 0 is a speaker block, column 1 a microphone block. The rows of one device (aligned blocks of 26 rows) all lie in that device's bin, and their speaker blocks s satisfy s // 2 = (device index) % 16; no pair repeats on a device. Counting microphone blocks m by the device m * 16 // 128, at most 4 rows of one device fall to any one device, and in every part one device gets exactly 4 from every device.
All inputs are finite; a program needn't handle non-finite values.
Results may differ from a plain program's by a relative error of at most 0.0032.
Values may be sent and summed in bfloat16 or wider, within the bound.
A program may use at most 128 MiB of HBM per device.

v0:
```python
import jax
import jax.numpy as jnp
from jax import lax
from jax.sharding import PartitionSpec as P

SBLK = 32
MBLK = 128
SPEAKERS = 4096


reg_weight = 0.25


def complex_forward(plant, field_rows):
    halfway = field_rows.shape[-1] // 2
    product = jnp.einsum("tcij,tjk->tcik", plant, field_rows, preferred_element_type=jnp.float32)
    real_part = product[:, 0, :, :halfway] - product[:, 1, :, halfway:]
    imag_part = product[:, 0, :, halfway:] + product[:, 1, :, :halfway]
    return jnp.concatenate([real_part, imag_part], axis=-1)


def complex_adjoint(plant, field_rows):
    halfway = field_rows.shape[-1] // 2
    product = jnp.einsum("tcij,tik->tcjk", plant, field_rows, preferred_element_type=jnp.float32)
    real_part = product[:, 0, :, :halfway] + product[:, 1, :, halfway:]
    imag_part = product[:, 0, :, halfway:] - product[:, 1, :, :halfway]
    return jnp.concatenate([real_part, imag_part], axis=-1)


def per_device(direction, plant, tile_pairs, mic_weight):
    devices = lax.axis_size("spk")
    device_id = lax.axis_index("spk")
    unit_count = direction.shape[0]
    tile_count = plant.shape[0]
    block_size = direction.shape[1]
    field_width = direction.shape[2]
    groups_per_bin = SBLK // unit_count
    bin_count = devices // groups_per_bin
    peer_blocks = MBLK // devices
    mic_units = bin_count * peer_blocks
    my_bin = device_id // groups_per_bin
    local_unit = tile_pairs[:, 0] % unit_count
    mic_block = tile_pairs[:, 1]
    direction_rows = direction.astype(jnp.bfloat16)[local_unit]
    partial_field = complex_forward(plant, direction_rows)
    local_power = jnp.sum(jnp.square(plant.astype(jnp.float32)))
    power_terms = jnp.where(jnp.arange(bin_count) == my_bin, local_power, 0.0)
    bin_power = lax.psum(power_terms, "spk")
    weights_flat = mic_weight.reshape(mic_units, block_size)
    capacity = max(3, (2 * tile_count + devices - 1) // devices)
    target_peer = mic_block // peer_blocks
    peer_onehot = (target_peer[:, None] == jnp.arange(devices)[None, :]).astype(jnp.int32)
    running = jnp.cumsum(peer_onehot, axis=0)
    slot_rank = jnp.take_along_axis(running, target_peer[:, None], axis=1)[:, 0] - 1
    position = target_peer * capacity + slot_rank
    target_label = my_bin * peer_blocks + mic_block - target_peer * peer_blocks
    outgoing = (
        jnp.zeros((devices * capacity, block_size, field_width), jnp.float32)
        .at[position]
        .set(partial_field)
    )
    labels = jnp.full((devices * capacity,), mic_units, jnp.int32).at[position].set(target_label)
    labels_in = lax.all_to_all(
        labels.reshape(devices, capacity), "spk", split_axis=0, concat_axis=0, tiled=True
    )
    arrived = lax.all_to_all(
        outgoing.reshape(devices, capacity, block_size, field_width),
        "spk",
        split_axis=0,
        concat_axis=0,
        tiled=True,
    )
    flat_labels = labels_in.reshape(devices * capacity)
    pressure = jax.ops.segment_sum(
        arrived.reshape(devices * capacity, block_size, field_width),
        flat_labels,
        num_segments=mic_units + 1,
    )[:mic_units]
    weighted = (weights_flat[:, :, None] * pressure).astype(jnp.bfloat16)
    clipped = jnp.minimum(flat_labels, mic_units - 1)
    reply = weighted[clipped].reshape(devices, capacity, block_size, field_width)
    returned = lax.all_to_all(reply, "spk", split_axis=0, concat_axis=0, tiled=True)
    tile_weighted = returned.reshape(devices * capacity, block_size, field_width)[position]
    back_field = complex_adjoint(plant, tile_weighted)
    unit_onehot = (local_unit[:, None] == jnp.arange(unit_count)[None, :]).astype(jnp.float32)
    gram = jnp.einsum("tu,tjk->ujk", unit_onehot, back_field, precision=lax.Precision.HIGHEST)
    my_power = bin_power[my_bin]
    return gram + reg_weight * my_power / SPEAKERS * direction


def solution(mesh):
    placed = (
        P(("band", "spk"), None, None),
        P(("band", "spk"), None, None, None),
        P(("band", "spk"), None),
        P("band", "spk", None),
    )
    return jax.shard_map(
        per_device,
        mesh=mesh,
        in_specs=placed,
        out_specs=P(("band", "spk"), None, None),
        check_vma=False,
    )
```

profile of v0, /device:TPU:1, one launch (start us, length us, event | category | flops | bytes accessed | tf_op | source)
XLA Modules:
  0.0 209.4 jit_solution(8495858670104442344)
XLA Ops:
  0.0 0.0 copy-start
  0.0 0.8 fusion.16
  0.9 0.7 fusion.18
  1.5 0.1 fusion.9
  1.7 0.8 gather_fusion.3
  2.5 0.7 scatter_custom_fusion
  3.2 0.7 all_to_all.12
  3.9 7.3 %all-to-all-start = ((s32[16,1,4]{2,1,0:T(1,128)}), s32[16,1,4]{2,1,0:T(1,128)S(1)}, u32[]{:S(2)}, u32[]{:S(2)}) async-start(s32[16,1,4]{2,1,0:T(1,128)} %bitcast.10), calls=%async_computation | async-start | bytes 16384 | tf_op jit(solution)/shard_map/all_to_all | solution.py:63
  11.2 0.9 convert_element_type.14
  12.1 0.7 gather_fusion
  12.8 0.0 copy-done
  12.9 0.7 convolution_bitcast_fusion.1
  13.5 0.1 fusion.3
  13.6 0.1 fusion.5
  13.8 0.2 pad_maximum_fusion
  14.0 1.7 copy.38
  15.6 0.0 copy-start.1
  15.6 2.4 %broadcast_in_dim.9 = f32[64,128,128]{2,1,0:T(8,128)} broadcast(f32[]{:T(128)} %constant.79.clone.1), dimensions={} | broadcast | bytes 4194308 | tf_op jit(solution)/shard_map/broadcast_in_dim | solution.py:58
  18.1 0.0 copy-done.1
  18.1 5.3 %scatter_fusion = f32[64,128,128]{2,1,0:T(8,128)} fusion(f32[64,128,128]{2,1,0:T(8,128)} %broadcast_in_dim.9, s32[26]{0:T(128)S(1)} %fusion.15, f32[26,128,128]{2,1,0:T(8,128)S(1)} %copy-done.1), kind=kCustom, calls=%fused_computation.5 | custom fusion | bytes 5111912 | tf_op jit(solution)/shard_map/scatter | solution.py:60
  23.4 0.0 all-to-all-done
  23.4 6.1 %all-to-all-start.1 = ((f32[16,4,128,128]{3,2,1,0:T(8,128)}), f32[16,4,128,128]{3,2,1,0:T(8,128)}, u32[]{:S(2)}, u32[]{:S(2)}) async-start(f32[16,4,128,128]{3,2,1,0:T(8,128)} %bitcast.87), calls=%async_computation.1 | async-start | bytes 8388608 | tf_op jit(solution)/shard_map/all_to_all | solution.py:66
  29.4 0.5 broadcast.181
  30.0 0.7 minimum_reduce_fusion
  30.7 0.1 reshape.124
  30.7 0.1 reshape.132
  30.9 76.7 %all-to-all-done.1 = f32[16,4,128,128]{3,2,1,0:T(8,128)} async-done(((f32[16,4,128,128]{3,2,1,0:T(8,128)}), f32[16,4,128,128]{3,2,1,0:T(8,128)}, u32[]{:S(2)}, u32[]{:S(2)}) %all-to-all-start.1) | async-done | bytes 4194336 | tf_op jit(solution)/shard_map/all_to_all | solution.py:66
  107.6 0.0 copy-start.3
  107.6 8.8 %scatter_fusion.1 = f32[9,128,128]{2,1,0:T(8,128)S(1)} fusion(f32[9,128,128]{2,1,0:T(8,128)S(1)} %broadcast_in_dim.8, s32[64]{0:T(128)S(1)} %reshape.124, f32[64,128,128]{2,1,0:T(8,128)} %bitcast.17), kind=kCustom, calls=%fused_computation.6 | custom fusion | flops 1048576 | bytes 12583168 | tf_op jit(solution)/shard_map/scatter-add | solution.py:74
  116.4 0.0 copy-done.3
  116.4 0.2 fusion.8
  116.6 2.1 %gather_fusion.1 = bf16[64,128,128]{2,1,0:T(8,128)(2,1)} fusion(bf16[8,128,128]{2,1,0:T(8,128)(2,1)S(1)} %fusion.8, s32[1024]{0:T(1024)S(1)} %pad_clamp_fusion.1), kind=kCustom, calls=%fused_computation.1 | custom fusion | bytes 4194560 | tf_op jit(solution)/shard_map/gather | solution.py:81
  118.7 19.3 %all-to-all-start.2 = ((bf16[16,4,128,128]{3,2,1,0:T(8,128)(2,1)}), bf16[16,4,128,128]{3,2,1,0:T(8,128)(2,1)}, u32[]{:S(2)}, u32[]{:S(2)}) async-start(bf16[16,4,128,128]{3,2,1,0:T(8,128)(2,1)} %bitcast.88), calls=%async_computation.2 | async-start | bytes 4194304 | tf_op jit(solution)/shard_map/all_to_all | solution.py:82
  138.0 1.5 multiply_reduce_fusion
  140.1 60.0 %psum.7 = f32[1]{0:T(128)} all-reduce(f32[1]{0:T(128)} %bitcast.25), channel_id=1, replica_groups=mesh['band'=2,'spk'=16] {'spk'}, use_global_device_ids=true, to_apply=%region_5.6 | all-reduce | flops 1 | bytes 8 | tf_op jit(solution)/shard_map/psum | solution.py:48
  200.8 0.0 all-to-all-done.2
  200.8 2.3 %gather_fusion.2 = bf16[26,128,128]{2,1,0:T(8,128)(2,1)S(1)} fusion(bf16[64,128,128]{2,1,0:T(8,128)(2,1)} %bitcast.20, s32[1024]{0:T(1024)S(1)} %pad_clamp_fusion), kind=kCustom, calls=%fused_computation.2 | custom fusion | bytes 1704040 | tf_op jit(solution)/shard_map/gather | solution.py:83
  203.1 0.7 convolution_bitcast_fusion
  203.7 0.1 fusion
  203.9 0.1 fusion.2
  204.0 0.1 pad_maximum_fusion.1
  204.1 0.0 copy-start.2
  204.1 2.2 %copy.42 = f32[26,128,128]{2,0,1:T(8,128)} copy(f32[26,128,128]{1,2,0:T(8,128)S(1)} %pad_maximum_fusion.1) | data formatting | bytes 3407872 | tf_op jit(solution)/shard_map/concatenate | solution.py:27
  206.4 2.4 %fusion.10 = f32[2,128,128]{2,0,1:T(2,128)S(1)} fusion(f32[26,128,128]{2,0,1:T(8,128)} %copy.42, s32[26]{0:T(128)S(1)} %bitcast.90), kind=kOutput, calls=%fused_computation.41 | convolution fusion | flops 10223668 | bytes 1835112 | tf_op jit(solution)/shard_map/tu,tjk->ujk/dot_general | solution.py:86
  208.7 0.0 copy-done.2
  208.7 0.7 copy_add_fusion
  (10 shorter events, 0.1 us)
Async XLA Ops:
  0.0 12.9 %copy-start = (bf16[26,2,128,128]{3,2,1,0:T(8,128)(2,1)S(1)}, bf16[26,2,128,128]{3,2,1,0:T(8,128)(2,1)}, u32[]{:S(2)}) copy-start(bf16[26,2,128,128]{3,2,1,0:T(8,128)(2,1)} %param.5) | copy-start | bytes 5111812
  3.9 19.5 %all-to-all-start = ((s32[16,1,4]{2,1,0:T(1,128)}), s32[16,1,4]{2,1,0:T(1,128)S(1)}, u32[]{:S(2)}, u32[]{:S(2)}) async-start(s32[16,1,4]{2,1,0:T(1,128)} %bitcast.10), calls=%async_computation | async-start | bytes 16384 | tf_op jit(solution)/shard_map/all_to_all | solution.py:63
  15.6 2.4 %copy-start.1 = (f32[26,128,128]{2,1,0:T(8,128)S(1)}, f32[26,128,128]{2,1,0:T(8,128)}, u32[]{:S(2)}) copy-start(f32[26,128,128]{2,1,0:T(8,128)} %copy.38) | copy-start | bytes 5111812
  23.4 84.1 %all-to-all-start.1 = ((f32[16,4,128,128]{3,2,1,0:T(8,128)}), f32[16,4,128,128]{3,2,1,0:T(8,128)}, u32[]{:S(2)}, u32[]{:S(2)}) async-start(f32[16,4,128,128]{3,2,1,0:T(8,128)} %bitcast.87), calls=%async_computation.1 | async-start | bytes 8388608 | tf_op jit(solution)/shard_map/all_to_all | solution.py:66
  107.6 8.8 %copy-start.3 = (f32[1,8,128]{2,1,0:T(8,128)S(1)}, f32[1,8,128]{2,1,0:T(8,128)}, u32[]{:S(2)}) copy-start(f32[1,8,128]{2,1,0:T(8,128)} %param.7) | copy-start | bytes 12292
  118.7 82.1 %all-to-all-start.2 = ((bf16[16,4,128,128]{3,2,1,0:T(8,128)(2,1)}), bf16[16,4,128,128]{3,2,1,0:T(8,128)(2,1)}, u32[]{:S(2)}, u32[]{:S(2)}) async-start(bf16[16,4,128,128]{3,2,1,0:T(8,128)(2,1)} %bitcast.88), calls=%async_computation.2 | async-start | bytes 4194304 | tf_op jit(solution)/shard_map/all_to_all | solution.py:82
  204.1 4.6 %copy-start.2 = (f32[2,128,128]{2,1,0:T(8,128)S(1)}, f32[2,128,128]{2,1,0:T(8,128)}, u32[]{:S(2)}) copy-start(f32[2,128,128]{2,1,0:T(8,128)} %param.4) | copy-start | bytes 393220
where the time goes:
time: 213 us; the launch traced here: 209 us
  waiting for transfers between devices  76.7 us (36%)
  blocking collectives  60 us (28%)
  starting transfers between devices  32.7 us (15%)
  local copies, waits for them, and re-layouts  19.6 us (9%)
  other arithmetic  15.2 us (7%)
  matrix products  3.66 us (2%)
    all_to_all x1, waiting for transfers between devices, per_device(): lax.all_to_all(outgoing.reshape(devices, capacity, block_size, field_widt...  76.7 us
    psum x1, blocking collectives, per_device(): bin_power = lax.psum(power_terms, 'spk')  60 us
    all_to_all x1, starting transfers between devices, per_device(): lax.all_to_all(reply, 'spk', split_axis=0, concat_axis=0, tiled=True)  19.3 us
    scatter-add x1, other arithmetic, per_device(): jax.ops.segment_sum(arrived.reshape(devices * capacity, block_size, field...  8.78 us
    all_to_all x1, starting transfers between devices, per_device(): lax.all_to_all(labels.reshape(devices, capacity), 'spk', split_axis=0, co...  7.35 us
    all_to_all x1, starting transfers between devices, per_device(): lax.all_to_all(outgoing.reshape(devices, capacity, block_size, field_widt...  6.06 us
    scatter x1, local copies, waits for them, and re-layouts, per_device(): outgoing = jnp.zeros((devices * capacity, block_size, field_width), jnp.f...  5.32 us
  transfers between devices with their start and end apart: 3, of which 1 were waited for; matrix products, arithmetic and copies ran while one was open for 7% of the time, Pallas kernels for 0%

commit v1 on v0

v1 whole, which is shorter than its diff:
```python
import functools

import jax
import jax.numpy as jnp
from jax import lax
from jax.experimental import pallas as pl
from jax.experimental.pallas import tpu as pltpu
from jax.sharding import PartitionSpec as P

SBLK = 32
MBLK = 128
SPEAKERS = 4096
CHUNK = 2

reg_weight = 0.25

MESH = pl.DeviceIdType.MESH


def kernel(
    group, fwd_idx, back_idx, direction, plant, weights, out,
    info, packed, flipped, fields, sib_out, sib_in, own, y_out, y_in,
    right_out, left_out, from_left, from_right, weighted, stacked,
    info_s, info_r, sib_s, sib_r, y_s, y_r, right_s, right_r, left_s, left_r,
    ws_s, ws_r, wy_s, wy_r, wf_s, wf_r,
):
    units, block, width = direction.shape
    tiles = plant.shape[0]
    quarter = MBLK // 4
    chunks = quarter // CHUNK
    rows_per = MBLK // group
    depth = group // 4
    half = width // 2

    me = lax.axis_index("spk")
    base = (me // group) * group
    rank = me - base
    z = rank // 4
    y = (rank // 2) % 2
    c = rank % 2
    sib = me + 1 - 2 * c
    other_y = me + 2 - 4 * y
    q_mine = y * 2 + c
    q_sib = y * 2 + 1 - c
    q_y = (1 - y) * 2 + c
    q_diag = (1 - y) * 2 + 1 - c
    has_left = z > 0
    has_right = z < depth - 1

    def peer(j):
        return base + (rank + j) % group

    def copy(src, dst, send, recv, device):
        return pltpu.make_async_remote_copy(
            src_ref=src, dst_ref=dst, send_sem=send, recv_sem=recv,
            device_id={"spk": device}, device_id_type=MESH,
        )

    barrier = pltpu.get_barrier_semaphore()
    for j in range(1, group):
        pl.semaphore_signal(barrier, inc=1, device_id={"spk": peer(j)}, device_id_type=MESH)

    lane = lax.broadcasted_iota(jnp.int32, (block, width), 1)
    for u in range(units):
        x = direction[u]
        turned = pltpu.roll(x, half, 1)
        turned = jnp.where(lane < half, -turned, turned)
        fields[u, :block, :] = x.astype(jnp.bfloat16)
        fields[u, block:, :] = turned.astype(jnp.bfloat16)

    def pack(t, power):
        p0 = plant[t, 0]
        p1 = plant[t, 1]
        packed[t, :, :block] = p0
        packed[t, :, block:] = p1
        f0 = p0.astype(jnp.float32)
        f1 = p1.astype(jnp.float32)
        squares = f0 * f0 + f1 * f1
        return power + jnp.sum(squares.reshape(block // 8, 8, block), axis=0)

    power = lax.fori_loop(0, tiles, pack, jnp.zeros((8, block), jnp.float32))
    packed[tiles] = jnp.zeros((block, 2 * block), jnp.bfloat16)
    weighted[MBLK] = jnp.zeros((block, width), jnp.bfloat16)
    info[rank, :rows_per, :] = weights[...]
    info[rank, rows_per:, :] = power

    pl.semaphore_wait(barrier, group - 1)

    def info_copy(j):
        return copy(info.at[rank], info.at[rank], info_s.at[j], info_r.at[j], peer(j))

    def sib_copy(k):
        return copy(sib_out.at[k], sib_in.at[k], sib_s.at[k], sib_r.at[k], sib)

    def y_copy(k):
        return copy(y_out.at[k], y_in.at[k], y_s.at[k], y_r.at[k], other_y)

    def right_copy(k):
        return copy(right_out.at[k], from_left.at[k], right_s.at[k], right_r.at[k], me + 4)

    def left_copy(k):
        return copy(left_out.at[k], from_right.at[k], left_s.at[k], left_r.at[k], me - 4)

    def part(q, k):
        return weighted.at[pl.ds(q * quarter + k * CHUNK, CHUNK)]

    def ws_copy(k):
        return copy(part(q_mine, k), part(q_mine, k), ws_s.at[k], ws_r.at[k], sib)

    def wy_copy(k):
        return copy(part(q_mine, k), part(q_mine, k), wy_s.at[k], wy_r.at[k], other_y)

    def wf_copy(k):
        return copy(part(q_y, k), part(q_y, k), wf_s.at[k], wf_r.at[k], sib)

    for j in range(1, group):
        info_copy(j).start()

    def product(v):
        total = jnp.dot(packed[fwd_idx[v * units]], fields[0], preferred_element_type=jnp.float32)
        for u in range(1, units):
            total += jnp.dot(
                packed[fwd_idx[v * units + u]], fields[u], preferred_element_type=jnp.float32
            )
        return total

    def inside(k):
        return jnp.logical_and(k >= 0, k < chunks)

    def step(s, carry):
        @pl.when(inside(s))
        def _():
            k = s
            for i in range(CHUNK):
                at = k * CHUNK + i
                sib_out[k, i] = product(q_sib * quarter + at).astype(jnp.bfloat16)
                sib_out[k, CHUNK + i] = product(q_diag * quarter + at).astype(jnp.bfloat16)
            sib_copy(k).start()
            for i in range(CHUNK):
                at = k * CHUNK + i
                own[k, i] = product(q_mine * quarter + at)
                own[k, CHUNK + i] = product(q_y * quarter + at)

        k1 = s - 1

        @pl.when(inside(k1))
        def _():
            sib_copy(k1).wait_recv()
            for i in range(CHUNK):
                total = own[k1, CHUNK + i] + sib_in[k1, CHUNK + i].astype(jnp.float32)
                y_out[k1, i] = total.astype(jnp.bfloat16)
            y_copy(k1).start()
            for i in range(CHUNK):
                own[k1, i] = own[k1, i] + sib_in[k1, i].astype(jnp.float32)

        k2 = s - 2

        @pl.when(inside(k2))
        def _():
            y_copy(k2).wait_recv()
            for i in range(CHUNK):
                own[k2, i] = own[k2, i] + y_in[k2, i].astype(jnp.float32)

        kr = s - 2 - z

        @pl.when(inside(kr))
        def _():
            @pl.when(has_left)
            def _():
                right_copy(kr).wait_recv()

            @pl.when(jnp.logical_and(has_left, has_right))
            def _():
                for i in range(CHUNK):
                    total = own[kr, i] + from_left[kr, i].astype(jnp.float32)
                    right_out[kr, i] = total.astype(jnp.bfloat16)

            @pl.when(jnp.logical_not(has_left))
            def _():
                for i in range(CHUNK):
                    right_out[kr, i] = own[kr, i].astype(jnp.bfloat16)

            @pl.when(has_right)
            def _():
                right_copy(kr).start()

        kl = s - 2 - (depth - 1 - z)

        @pl.when(inside(kl))
        def _():
            @pl.when(has_right)
            def _():
                left_copy(kl).wait_recv()

            @pl.when(jnp.logical_and(has_left, has_right))
            def _():
                for i in range(CHUNK):
                    total = own[kl, i] + from_right[kl, i].astype(jnp.float32)
                    left_out[kl, i] = total.astype(jnp.bfloat16)

            @pl.when(jnp.logical_not(has_right))
            def _():
                for i in range(CHUNK):
                    left_out[kl, i] = own[kl, i].astype(jnp.bfloat16)

            @pl.when(has_left)
            def _():
                left_copy(kl).start()

        kt = s - 2 - jnp.maximum(z, depth - 1 - z)

        @pl.when(kt == 0)
        def _():
            for j in range(1, group):
                info_copy(j).wait_recv()

        @pl.when(inside(kt))
        def _():
            @pl.when(has_left)
            def _():
                for i in range(CHUNK):
                    own[kt, i] = own[kt, i] + from_left[kt, i].astype(jnp.float32)

            @pl.when(has_right)
            def _():
                for i in range(CHUNK):
                    own[kt, i] = own[kt, i] + from_right[kt, i].astype(jnp.float32)

            for i in range(CHUNK):
                v = q_mine * quarter + kt * CHUNK + i
                row = info[v // rows_per, pl.ds(v % rows_per, 1), :]
                scale = jnp.broadcast_to(row, (block, block)).T
                weighted[v] = (scale * own[kt, i]).astype(jnp.bfloat16)
            wy_copy(kt).start()
            ws_copy(kt).start()

        kd = kt - 1

        @pl.when(inside(kd))
        def _():
            wy_copy(kd).wait_recv()
            wf_copy(kd).start()

        for n in range(2):
            t = s * 2 + n

            @pl.when(t < tiles)
            def _():
                flipped[t, :block, :] = plant[t, 0].T
                flipped[t, block:, :] = plant[t, 1].T

        return carry

    steps = max(chunks + 3 + depth - 1, (tiles + 1) // 2)
    lax.fori_loop(0, steps, step, 0)

    def arrived(k, carry):
        ws_copy(k).wait_recv()
        wf_copy(k).wait_recv()
        return carry

    lax.fori_loop(0, chunks, arrived, 0)

    for t in range(tiles):
        for u in range(units):
            stacked[t, :, u * width:(u + 1) * width] = weighted[back_idx[t * units + u]]
    total = jnp.zeros((2 * block, units * width), jnp.float32)
    for t in range(tiles):
        total += jnp.dot(flipped[t], stacked[t], preferred_element_type=jnp.float32)

    power_sum = jnp.sum(info[:, rows_per:, :], axis=0)
    power_sum = jnp.sum(jnp.sum(power_sum, axis=1, keepdims=True), axis=0, keepdims=True)
    coefficient = reg_weight * power_sum / SPEAKERS
    for u in range(units):
        straight = total[:block, u * width:(u + 1) * width]
        crossed = pltpu.roll(total[block:, u * width:(u + 1) * width], half, 1)
        crossed = jnp.where(lane < half, crossed, -crossed)
        out[u] = straight + crossed + coefficient * direction[u]

    for j in range(1, group):
        info_copy(j).wait_send()

    def sent(k, carry):
        sib_copy(k).wait_send()
        y_copy(k).wait_send()
        ws_copy(k).wait_send()
        wy_copy(k).wait_send()
        wf_copy(k).wait_send()

        @pl.when(has_right)
        def _():
            right_copy(k).wait_send()

        @pl.when(has_left)
        def _():
            left_copy(k).wait_send()

        return carry

    lax.fori_loop(0, chunks, sent, 0)


def per_device(direction, plant, tile_pairs, mic_weight):
    device_id = lax.axis_index("spk")
    units, block, width = direction.shape
    tiles = plant.shape[0]
    bins = mic_weight.shape[0]
    group = SBLK // units
    quarter = MBLK // 4
    chunks = quarter // CHUNK
    rows_per = MBLK // group

    if bins == 1:
        weights = mic_weight.reshape(rows_per, block)
    else:
        whole = lax.all_gather(mic_weight, "spk", axis=1, tiled=True)
        weights = lax.dynamic_slice(
            whole, (device_id // group, (device_id % group) * rows_per, 0), (1, rows_per, block)
        )[0]

    unit = tile_pairs[:, 0] % units
    mic = tile_pairs[:, 1]
    unit_hit = unit[:, None] == jnp.arange(units, dtype=jnp.int32)[None, :]
    mic_hit = mic[:, None] == jnp.arange(MBLK, dtype=jnp.int32)[None, :]
    both = jnp.logical_and(mic_hit[:, :, None], unit_hit[:, None, :])
    order = tiles - jnp.arange(tiles, dtype=jnp.int32)
    fwd_idx = tiles - jnp.sum(jnp.where(both, order[:, None, None], 0), axis=0)
    back_idx = jnp.where(unit_hit, mic[:, None], MBLK)

    bf16, f32 = jnp.bfloat16, jnp.float32
    dma = pltpu.SemaphoreType.DMA
    vmem = pl.BlockSpec(memory_space=pltpu.VMEM)
    smem = pl.BlockSpec(memory_space=pltpu.SMEM)
    piece = (chunks, CHUNK, block, width)
    double = (chunks, 2 * CHUNK, block, width)
    return pl.pallas_call(
        functools.partial(kernel, group),
        out_shape=jax.ShapeDtypeStruct(direction.shape, f32),
        in_specs=[smem, smem, vmem, vmem, vmem],
        out_specs=vmem,
        scratch_shapes=[
            pltpu.VMEM((group, rows_per + 8, block), f32),
            pltpu.VMEM((tiles + 1, block, 2 * block), bf16),
            pltpu.VMEM((tiles, 2 * block, block), bf16),
            pltpu.VMEM((units, 2 * block, width), bf16),
            pltpu.VMEM(double, bf16),
            pltpu.VMEM(double, bf16),
            pltpu.VMEM(double, f32),
            pltpu.VMEM(piece, bf16),
            pltpu.VMEM(piece, bf16),
            pltpu.VMEM(piece, bf16),
            pltpu.VMEM(piece, bf16),
            pltpu.VMEM(piece, bf16),
            pltpu.VMEM(piece, bf16),
            pltpu.VMEM((MBLK + 1, block, width), bf16),
            pltpu.VMEM((tiles, block, units * width), bf16),
            dma((group,)), dma((group,)),
        ] + [dma((chunks,)) for _ in range(14)],
        compiler_params=pltpu.CompilerParams(
            collective_id=0, has_side_effects=True, vmem_limit_bytes=48 * 1024 * 1024
        ),
        name="pressure_matching",
    )(fwd_idx.reshape(-1), back_idx.reshape(-1), direction, plant, weights)


def solution(mesh):
    placed = (
        P(("band", "spk"), None, None),
        P(("band", "spk"), None, None, None),
        P(("band", "spk"), None),
        P("band", "spk", None),
    )
    return jax.shard_map(
        per_device,
        mesh=mesh,
        in_specs=placed,
        out_specs=P(("band", "spk"), None, None),
        check_vma=False,
    )
```

time: 213 us -> 82.8 us (0.39); the launches traced: 209 us -> 82.6 us
  Pallas kernels: 0 us -> 77.4 us
  waiting for transfers between devices: 76.7 us -> 0 us
  blocking collectives: 60 us -> 0 us
  starting transfers between devices: 32.7 us -> 0 us
  local copies, waits for them, and re-layouts: 19.6 us -> 4.05 us
  other arithmetic: 15.2 us -> 1.12 us
  matrix products: 3.66 us -> 0 us
    pallas_call x0 -> x1, Pallas kernels: none -> 77.4 us  [per_device(): pl.pallas_call(functools.partial(kernel, group), out_shape=jax.ShapeDtype...]
    all_to_all x3 -> x0, waiting for transfers between devices: 76.7 us -> none  [the longest x1 76.7 us: per_device(): lax.all_to_all(outgoing.reshape(devices, capacity, block_size, field_widt...]
    psum x1 -> x0, blocking collectives: 60 us -> none  [per_device(): bin_power = lax.psum(power_terms, 'spk')]
    all_to_all x3 -> x0, starting transfers between devices: 32.7 us -> none  [the longest x1 19.3 us: per_device(): lax.all_to_all(reply, 'spk', split_axis=0, concat_axis=0, tiled=True)]
    scatter-add x1 -> x0, other arithmetic: 8.78 us -> none  [per_device(): jax.ops.segment_sum(arrived.reshape(devices * capacity, block_size, field...]
    scatter x2 -> x0, local copies, waits for them, and re-layouts: 5.97 us -> none  [the longest x1 5.32 us: per_device(): outgoing = jnp.zeros((devices * capacity, block_size, field_width), jnp.f...]
    gather x4 -> x0, local copies, waits for them, and re-layouts: 5.91 us -> none  [the longest x1 2.3 us: per_device(): returned.reshape(devices * capacity, block_size, field_width)[position]]
    concatenate x2 -> x0, local copies, waits for them, and re-layouts: 3.88 us -> none  [the longest x1 2.22 us: complex_adjoint(): return jnp.concatenate([real_part, imag_part], axis=-1)]
  transfers between devices with their start and end apart: 3 -> 0, of which waited for: 1 -> 0; matrix products, arithmetic and copies ran while one was open for 7% -> 0% of each run, Pallas kernels for 0% -> 0%
where the time goes in v1:
time: 82.8 us; the launch traced here: 82.6 us
  Pallas kernels  77.4 us (93%)
  local copies, waits for them, and re-layouts  4.05 us (5%)
  other arithmetic  1.12 us (1%)
    pallas_call x1, Pallas kernels, per_device(): pl.pallas_call(functools.partial(kernel, group), out_shape=jax.ShapeDtype...  77.4 us
    unnamed x7, local copies, waits for them, and re-layouts  3.7 us

profile of v1, /device:TPU:1, one launch (start us, length us, event | category | flops | bytes accessed | tf_op | source)
XLA Modules:
  0.0 82.6 jit_solution(2465505623731331029)
XLA Ops:
  0.0 0.8 slice_bitcast_fusion
  0.8 0.1 iota_compare_fusion.1
  0.8 0.1 iota_compare_fusion
  0.9 0.1 fusion
  1.1 0.1 broadcast_select_fusion
  1.1 0.1 select_n.23.back_idx
  1.2 0.1 copy.5
  1.4 0.1 sub.20.fwd_idx
  1.5 0.0 copy-start
  1.5 1.4 %copy-done = bf16[26,2,128,128]{3,2,1,0:T(8,128)(2,1)S(1)} copy-done((bf16[26,2,128,128]{3,2,1,0:T(8,128)(2,1)S(1)}, bf16[26,2,128,128]{3,2,1,0:T(8,128)(2,1)}, u32[]{:S(2)}) %copy-start) | copy-done | bytes 1703960
  3.0 0.0 copy-start.1
  3.0 0.9 %copy-done.1 = f32[2,128,128]{2,1,0:T(8,128)S(1)} copy-done((f32[2,128,128]{2,1,0:T(8,128)S(1)}, f32[2,128,128]{2,1,0:T(8,128)}, u32[]{:S(2)}) %copy-start.1) | copy-done | bytes 131096
  3.9 0.0 copy-start.2
  3.9 0.7 copy-done.2
  4.5 77.4 %pressure_matching.1 = f32[2,128,128]{2,1,0:T(8,128)S(1)} custom-call(s32[256]{0:T(256)S(1)} %sub.20.fwd_idx, s32[52]{0:T(128)S(1)} %select_n.23.back_idx, f32[2,128,128]{2,1,0:T(8,128)S(1)} %copy-done.1, bf16[26,2,128,128]{3,2,1,0:T(8,128)(2,1)S(1)} %copy-done, f32[8,128]{1,0:T(8,128)S(1)} %bitcast.5), custom_call_target="tpu_custom_call" | custom-call | tf_op jit(solution)/shard_map/pressure_matching/pallas_call | solution.py:336
  82.0 0.7 copy.7
  (2 shorter events, 0.0 us)
Async XLA Ops:
  1.5 1.5 %copy-start = (bf16[26,2,128,128]{3,2,1,0:T(8,128)(2,1)S(1)}, bf16[26,2,128,128]{3,2,1,0:T(8,128)(2,1)}, u32[]{:S(2)}) copy-start(bf16[26,2,128,128]{3,2,1,0:T(8,128)(2,1)} %plant.1) | copy-start | bytes 5111812
  3.0 0.9 %copy-start.1 = (f32[2,128,128]{2,1,0:T(8,128)S(1)}, f32[2,128,128]{2,1,0:T(8,128)}, u32[]{:S(2)}) copy-start(f32[2,128,128]{2,1,0:T(8,128)} %direction.1) | copy-start | bytes 393220
  3.9 0.7 copy-start.2

commit v2 on v1

--- a/solution.py
+++ b/solution.py
@@ -18,10 +18,10 @@
 
 
 def kernel(
-    group, fwd_idx, back_idx, direction, plant, weights, out,
-    info, packed, flipped, fields, sib_out, sib_in, own, y_out, y_in,
+    group, fwd_idx, pair_key, direction_in, plant_in, weights_in, out,
+    direction, plant, weights, info, products, flipped, fields, sib_out, sib_in, own, y_out, y_in,
     right_out, left_out, from_left, from_right, weighted, stacked,
-    info_s, info_r, sib_s, sib_r, y_s, y_r, right_s, right_r, left_s, left_r,
+    load_s, info_s, info_r, sib_s, sib_r, y_s, y_r, right_s, right_r, left_s, left_r,
     ws_s, ws_r, wy_s, wy_r, wf_s, wf_r,
 ):
     units, block, width = direction.shape
@@ -56,31 +56,45 @@
             device_id={"spk": device}, device_id_type=MESH,
         )
 
+    loads = [
+        pltpu.make_async_copy(src, dst, load_s.at[n])
+        for n, (src, dst) in enumerate(
+            [(direction_in, direction), (plant_in, plant), (weights_in, weights)]
+        )
+    ]
+    for load in loads:
+        load.start()
     barrier = pltpu.get_barrier_semaphore()
     for j in range(1, group):
         pl.semaphore_signal(barrier, inc=1, device_id={"spk": peer(j)}, device_id_type=MESH)
 
+    loads[0].wait()
     lane = lax.broadcasted_iota(jnp.int32, (block, width), 1)
     for u in range(units):
         x = direction[u]
         turned = pltpu.roll(x, half, 1)
         turned = jnp.where(lane < half, -turned, turned)
-        fields[u, :block, :] = x.astype(jnp.bfloat16)
-        fields[u, block:, :] = turned.astype(jnp.bfloat16)
+        fields[:block, u * width:(u + 1) * width] = x.astype(jnp.bfloat16)
+        fields[block:, u * width:(u + 1) * width] = turned.astype(jnp.bfloat16)
+    loads[1].wait()
 
     def pack(t, power):
         p0 = plant[t, 0]
         p1 = plant[t, 1]
-        packed[t, :, :block] = p0
-        packed[t, :, block:] = p1
+        both = jnp.dot(
+            jnp.concatenate([p0, p1], axis=1), fields[...], preferred_element_type=jnp.float32
+        )
+        for u in range(units):
+            products[t * units + u] = both[:, u * width:(u + 1) * width]
         f0 = p0.astype(jnp.float32)
         f1 = p1.astype(jnp.float32)
         squares = f0 * f0 + f1 * f1
         return power + jnp.sum(squares.reshape(block // 8, 8, block), axis=0)
 
     power = lax.fori_loop(0, tiles, pack, jnp.zeros((8, block), jnp.float32))
-    packed[tiles] = jnp.zeros((block, 2 * block), jnp.bfloat16)
+    products[tiles * units] = jnp.zeros((block, width), jnp.float32)
     weighted[MBLK] = jnp.zeros((block, width), jnp.bfloat16)
+    loads[2].wait()
     info[rank, :rows_per, :] = weights[...]
     info[rank, rows_per:, :] = power
 
@@ -117,11 +131,9 @@
         info_copy(j).start()
 
     def product(v):
-        total = jnp.dot(packed[fwd_idx[v * units]], fields[0], preferred_element_type=jnp.float32)
+        total = products[fwd_idx[v * units]]
         for u in range(1, units):
-            total += jnp.dot(
-                packed[fwd_idx[v * units + u]], fields[u], preferred_element_type=jnp.float32
-            )
+            total += products[fwd_idx[v * units + u]]
         return total
 
     def inside(k):
@@ -262,8 +274,10 @@
     lax.fori_loop(0, chunks, arrived, 0)
 
     for t in range(tiles):
+        key = pair_key[t]
         for u in range(units):
-            stacked[t, :, u * width:(u + 1) * width] = weighted[back_idx[t * units + u]]
+            at = jnp.where(key % units == u, key // units, MBLK)
+            stacked[t, :, u * width:(u + 1) * width] = weighted[at]
     total = jnp.zeros((2 * block, units * width), jnp.float32)
     for t in range(tiles):
         total += jnp.dot(flipped[t], stacked[t], preferred_element_type=jnp.float32)
@@ -319,30 +333,32 @@
         )[0]
 
     unit = tile_pairs[:, 0] % units
-    mic = tile_pairs[:, 1]
-    unit_hit = unit[:, None] == jnp.arange(units, dtype=jnp.int32)[None, :]
-    mic_hit = mic[:, None] == jnp.arange(MBLK, dtype=jnp.int32)[None, :]
-    both = jnp.logical_and(mic_hit[:, :, None], unit_hit[:, None, :])
-    order = tiles - jnp.arange(tiles, dtype=jnp.int32)
-    fwd_idx = tiles - jnp.sum(jnp.where(both, order[:, None, None], 0), axis=0)
-    back_idx = jnp.where(unit_hit, mic[:, None], MBLK)
+    pair_key = tile_pairs[:, 1] * units + unit
+    last = tiles * units
+    slot = jnp.arange(tiles, dtype=jnp.int32) * units + unit
+    hit = pair_key[:, None] == jnp.arange(MBLK * units, dtype=jnp.int32)[None, :]
+    fwd_idx = last - jnp.sum(jnp.where(hit, (last - slot)[:, None], 0), axis=0)
 
     bf16, f32 = jnp.bfloat16, jnp.float32
     dma = pltpu.SemaphoreType.DMA
     vmem = pl.BlockSpec(memory_space=pltpu.VMEM)
+    hbm = pl.BlockSpec(memory_space=pl.ANY)
     smem = pl.BlockSpec(memory_space=pltpu.SMEM)
     piece = (chunks, CHUNK, block, width)
     double = (chunks, 2 * CHUNK, block, width)
     return pl.pallas_call(
         functools.partial(kernel, group),
         out_shape=jax.ShapeDtypeStruct(direction.shape, f32),
-        in_specs=[smem, smem, vmem, vmem, vmem],
+        in_specs=[smem, smem, hbm, hbm, hbm],
         out_specs=vmem,
         scratch_shapes=[
+            pltpu.VMEM(direction.shape, f32),
+            pltpu.VMEM(plant.shape, bf16),
+            pltpu.VMEM(weights.shape, f32),
             pltpu.VMEM((group, rows_per + 8, block), f32),
-            pltpu.VMEM((tiles + 1, block, 2 * block), bf16),
+            pltpu.VMEM((tiles * units + 1, block, width), f32),
             pltpu.VMEM((tiles, 2 * block, block), bf16),
-            pltpu.VMEM((units, 2 * block, width), bf16),
+            pltpu.VMEM((2 * block, units * width), bf16),
             pltpu.VMEM(double, bf16),
             pltpu.VMEM(double, bf16),
             pltpu.VMEM(double, f32),
@@ -354,13 +370,13 @@
             pltpu.VMEM(piece, bf16),
             pltpu.VMEM((MBLK + 1, block, width), bf16),
             pltpu.VMEM((tiles, block, units * width), bf16),
-            dma((group,)), dma((group,)),
+            dma((3,)), dma((group,)), dma((group,)),
         ] + [dma((chunks,)) for _ in range(14)],
         compiler_params=pltpu.CompilerParams(
-            collective_id=0, has_side_effects=True, vmem_limit_bytes=48 * 1024 * 1024
+            collective_id=0, has_side_effects=True, vmem_limit_bytes=60 * 1024 * 1024
         ),
         name="pressure_matching",
-    )(fwd_idx.reshape(-1), back_idx.reshape(-1), direction, plant, weights)
+    )(fwd_idx, pair_key, direction, plant, weights)
 
 
 def solution(mesh):

time: 82.8 us -> 84.6 us (1.022)
  Pallas kernels: 77.4 us -> 80.1 us
  local copies, waits for them, and re-layouts: 4.05 us -> 1.57 us
  other arithmetic: 1.12 us -> 2.7 us
    pallas_call x1, Pallas kernels: 77.4 us -> 80.1 us  [per_device(): pl.pallas_call(functools.partial(kernel, group), out_shape=jax.ShapeDtype...]
    unnamed x7 -> x1, local copies, waits for them, and re-layouts: 3.7 us -> 1.57 us
    add x0 -> x1, other arithmetic: none -> 1.27 us  [per_device(): pair_key = tile_pairs[:, 1] * units + unit]
where the time goes in v2:
time: 84.6 us; the launch traced here: 84.4 us
  Pallas kernels  80.1 us (95%)
  other arithmetic  2.7 us (3%)
  local copies, waits for them, and re-layouts  1.57 us (2%)
    pallas_call x1, Pallas kernels, per_device(): pl.pallas_call(functools.partial(kernel, group), out_shape=jax.ShapeDtype...  80.1 us

profile of v2, /device:TPU:1, one launch (start us, length us, event | category | flops | bytes accessed | tf_op | source)
XLA Modules:
  0.0 84.4 jit_solution(16732784261897926824)
XLA Ops:
  0.0 1.3 %fusion.pair_key = s32[26]{0:T(128)} fusion(s32[26,2]{0,1:T(2,128)} %param.6), kind=kLoop, calls=%fused_computation.8 | loop fusion | flops 338 | bytes 312 | tf_op jit(solution)/shard_map/add | solution.py:336
  1.3 0.8 add_bitcast_fusion
  2.0 0.1 select_reduce_fusion
  2.1 0.6 broadcast_subtract_fusion.fwd_idx
  2.7 80.1 %pressure_matching.1 = f32[2,128,128]{2,1,0:T(8,128)} custom-call(s32[256]{0:T(256)} %broadcast_subtract_fusion.fwd_idx, s32[26]{0:T(128)} %fusion.pair_key, f32[2,128,128]{2,1,0:T(8,128)} %direction_in.1, bf16[26,2,128,128]{3,2,1,0:T(8,128)(2,1)} %plant_in.1, f32[8,128]{1,0:T(8,128)} %bitcast.9), custom_call_target="tpu_custom_call" | custom-call | tf_op jit(solution)/shard_map/pressure_matching/pallas_call | solution.py:349
  82.8 1.6 %copy.6 = f32[2,128,128]{2,1,0:T(8,128)} copy(f32[2,128,128]{2,1,0:T(8,128)} %pressure_matching.1) | data formatting | bytes 262144
  (1 shorter events, 0.0 us)

commit v3 on v2

--- a/solution.py
+++ b/solution.py
@@ -10,7 +10,8 @@
 SBLK = 32
 MBLK = 128
 SPEAKERS = 4096
-CHUNK = 2
+CHUNKS = 16
+LAG = 2
 
 reg_weight = 0.25
 
@@ -19,17 +20,21 @@
 
 def kernel(
     group, fwd_idx, pair_key, direction_in, plant_in, weights_in, out,
-    direction, plant, weights, info, products, flipped, fields, sib_out, sib_in, own, y_out, y_in,
-    right_out, left_out, from_left, from_right, weighted, stacked,
-    load_s, info_s, info_r, sib_s, sib_r, y_s, y_r, right_s, right_r, left_s, left_r,
-    ws_s, ws_r, wy_s, wy_r, wf_s, wf_r,
+    direction, plant, weights, info, products, flipped, fields, sib_out, sib_in, own,
+    y_out, y_in, right_out, left_out, from_left, from_right,
+    root_out, root_left, root_right, swap_out, swap_in, weighted, stacked,
+    load_s, info_s, info_r, sends,
+    sib_r, y_r, right_r, left_r, wy_r, toward_right_r, toward_left_r, swap_r, spread_r, ends_r,
 ):
     units, block, width = direction.shape
     tiles = plant.shape[0]
-    quarter = MBLK // 4
-    chunks = quarter // CHUNK
+    column = MBLK // 8
+    square = MBLK // 4
+    per_a = column // CHUNKS
+    per_b = square // CHUNKS
     rows_per = MBLK // group
     depth = group // 4
+    reach = depth // 2
     half = width // 2
 
     me = lax.axis_index("spk")
@@ -44,6 +49,8 @@
     q_sib = y * 2 + 1 - c
     q_y = (1 - y) * 2 + c
     q_diag = (1 - y) * 2 + 1 - c
+    wide_mine = MBLK // 2 + c * square
+    wide_sib = MBLK // 2 + (1 - c) * square
     has_left = z > 0
     has_right = z < depth - 1
 
@@ -103,29 +110,50 @@
     def info_copy(j):
         return copy(info.at[rank], info.at[rank], info_s.at[j], info_r.at[j], peer(j))
 
+    def part(q, k):
+        return weighted.at[pl.ds(q * column + k * per_a, per_a)]
+
+    def wide(first, k):
+        return weighted.at[pl.ds(first + k * per_b, per_b)]
+
     def sib_copy(k):
-        return copy(sib_out.at[k], sib_in.at[k], sib_s.at[k], sib_r.at[k], sib)
+        return copy(sib_out.at[k], sib_in.at[k], sends.at[0], sib_r.at[k], sib)
 
     def y_copy(k):
-        return copy(y_out.at[k], y_in.at[k], y_s.at[k], y_r.at[k], other_y)
+        return copy(y_out.at[k], y_in.at[k], sends.at[1], y_r.at[k], other_y)
 
     def right_copy(k):
-        return copy(right_out.at[k], from_left.at[k], right_s.at[k], right_r.at[k], me + 4)
+        return copy(right_out.at[k], from_left.at[k], sends.at[2], right_r.at[k], me + 4)
 
     def left_copy(k):
-        return copy(left_out.at[k], from_right.at[k], left_s.at[k], left_r.at[k], me - 4)
-
-    def part(q, k):
-        return weighted.at[pl.ds(q * quarter + k * CHUNK, CHUNK)]
+        return copy(left_out.at[k], from_right.at[k], sends.at[3], left_r.at[k], me - 4)
+
+    def wy_copy(k):
+        return copy(part(q_mine, k), part(q_mine, k), sends.at[4], wy_r.at[k], other_y)
 
     def ws_copy(k):
-        return copy(part(q_mine, k), part(q_mine, k), ws_s.at[k], ws_r.at[k], sib)
-
-    def wy_copy(k):
-        return copy(part(q_mine, k), part(q_mine, k), wy_s.at[k], wy_r.at[k], other_y)
+        return copy(part(q_mine, k), part(q_mine, k), sends.at[5], ends_r.at[0], sib)
 
     def wf_copy(k):
-        return copy(part(q_y, k), part(q_y, k), wf_s.at[k], wf_r.at[k], sib)
+        return copy(part(q_y, k), part(q_y, k), sends.at[6], ends_r.at[1], sib)
+
+    def wide_copy(k):
+        return copy(wide(wide_mine, k), wide(wide_mine, k), sends.at[7], ends_r.at[2], sib)
+
+    def toward_right(k):
+        return copy(root_out.at[k], root_left.at[k], sends.at[8], toward_right_r.at[k], me + 4)
+
+    def toward_left(k):
+        return copy(root_out.at[k], root_right.at[k], sends.at[9], toward_left_r.at[k], me - 4)
+
+    def swap_copy(k):
+        return copy(swap_out.at[k], swap_in.at[k], sends.at[10], swap_r.at[k], other_y)
+
+    def spread_right(k):
+        return copy(wide(wide_mine, k), wide(wide_mine, k), sends.at[11], spread_r.at[k], me + 4)
+
+    def spread_left(k):
+        return copy(wide(wide_mine, k), wide(wide_mine, k), sends.at[12], spread_r.at[k], me - 4)
 
     for j in range(1, group):
         info_copy(j).start()
@@ -137,43 +165,94 @@
         return total
 
     def inside(k):
-        return jnp.logical_and(k >= 0, k < chunks)
+        return jnp.logical_and(k >= 0, k < CHUNKS)
+
+    def scaled(v, pressure):
+        row = info[v // rows_per, pl.ds(v % rows_per, 1), :]
+        scale = jnp.broadcast_to(row, (block, block)).T
+        weighted[v] = (scale * pressure).astype(jnp.bfloat16)
+
+    def root_of(k):
+        return reach - 1 + k % 2
 
     def step(s, carry):
         @pl.when(inside(s))
         def _():
             k = s
-            for i in range(CHUNK):
-                at = k * CHUNK + i
-                sib_out[k, i] = product(q_sib * quarter + at).astype(jnp.bfloat16)
-                sib_out[k, CHUNK + i] = product(q_diag * quarter + at).astype(jnp.bfloat16)
+            for i in range(per_a):
+                at = k * per_a + i
+                sib_out[k, i] = product(q_sib * column + at).astype(jnp.bfloat16)
+                sib_out[k, per_a + i] = product(q_diag * column + at).astype(jnp.bfloat16)
+            for i in range(per_b):
+                at = k * per_b + i
+                sib_out[k, 2 * per_a + i] = product(wide_sib + at).astype(jnp.bfloat16)
             sib_copy(k).start()
-            for i in range(CHUNK):
-                at = k * CHUNK + i
-                own[k, i] = product(q_mine * quarter + at)
-                own[k, CHUNK + i] = product(q_y * quarter + at)
-
-        k1 = s - 1
+            for i in range(per_a):
+                at = k * per_a + i
+                own[k, i] = product(q_mine * column + at)
+                own[k, per_a + i] = product(q_y * column + at)
+            for i in range(per_b):
+                own[k, 2 * per_a + i] = product(wide_mine + k * per_b + i)
+
+        k1 = s - LAG
 
         @pl.when(inside(k1))
         def _():
             sib_copy(k1).wait_recv()
-            for i in range(CHUNK):
-                total = own[k1, CHUNK + i] + sib_in[k1, CHUNK + i].astype(jnp.float32)
+            for i in range(per_a):
+                total = own[k1, per_a + i] + sib_in[k1, per_a + i].astype(jnp.float32)
                 y_out[k1, i] = total.astype(jnp.bfloat16)
             y_copy(k1).start()
-            for i in range(CHUNK):
+            for i in range(per_a):
                 own[k1, i] = own[k1, i] + sib_in[k1, i].astype(jnp.float32)
-
-        k2 = s - 2
+            for i in range(2 * per_a, 2 * per_a + per_b):
+                own[k1, i] = own[k1, i] + sib_in[k1, i].astype(jnp.float32)
+
+        for d in range(reach, 0, -1):
+            kb = s - LAG * (1 + reach - d)
+            gap = z - root_of(kb)
+
+            @pl.when(jnp.logical_and(inside(kb), gap == -d))
+            def _():
+                @pl.when(has_left)
+                def _():
+                    toward_right(kb).wait_recv()
+                    for i in range(per_b):
+                        total = own[kb, 2 * per_a + i] + root_left[kb, i].astype(jnp.float32)
+                        root_out[kb, i] = total.astype(jnp.bfloat16)
+
+                @pl.when(jnp.logical_not(has_left))
+                def _():
+                    for i in range(per_b):
+                        root_out[kb, i] = own[kb, 2 * per_a + i].astype(jnp.bfloat16)
+
+                toward_right(kb).start()
+
+            @pl.when(jnp.logical_and(inside(kb), gap == d))
+            def _():
+                @pl.when(has_right)
+                def _():
+                    toward_left(kb).wait_recv()
+                    for i in range(per_b):
+                        total = own[kb, 2 * per_a + i] + root_right[kb, i].astype(jnp.float32)
+                        root_out[kb, i] = total.astype(jnp.bfloat16)
+
+                @pl.when(jnp.logical_not(has_right))
+                def _():
+                    for i in range(per_b):
+                        root_out[kb, i] = own[kb, 2 * per_a + i].astype(jnp.bfloat16)
+
+                toward_left(kb).start()
+
+        k2 = s - 2 * LAG
 
         @pl.when(inside(k2))
         def _():
             y_copy(k2).wait_recv()
-            for i in range(CHUNK):
+            for i in range(per_a):
                 own[k2, i] = own[k2, i] + y_in[k2, i].astype(jnp.float32)
 
-        kr = s - 2 - z
+        kr = s - LAG * (2 + z)
 
         @pl.when(inside(kr))
         def _():
@@ -183,20 +262,20 @@
 
             @pl.when(jnp.logical_and(has_left, has_right))
             def _():
-                for i in range(CHUNK):
+                for i in range(per_a):
                     total = own[kr, i] + from_left[kr, i].astype(jnp.float32)
                     right_out[kr, i] = total.astype(jnp.bfloat16)
 
             @pl.when(jnp.logical_not(has_left))
             def _():
-                for i in range(CHUNK):
+                for i in range(per_a):
                     right_out[kr, i] = own[kr, i].astype(jnp.bfloat16)
 
             @pl.when(has_right)
             def _():
                 right_copy(kr).start()
 
-        kl = s - 2 - (depth - 1 - z)
+        kl = s - LAG * (2 + depth - 1 - z)
 
         @pl.when(inside(kl))
         def _():
@@ -206,72 +285,137 @@
 
             @pl.when(jnp.logical_and(has_left, has_right))
             def _():
-                for i in range(CHUNK):
+                for i in range(per_a):
                     total = own[kl, i] + from_right[kl, i].astype(jnp.float32)
                     left_out[kl, i] = total.astype(jnp.bfloat16)
 
             @pl.when(jnp.logical_not(has_right))
             def _():
-                for i in range(CHUNK):
+                for i in range(per_a):
                     left_out[kl, i] = own[kl, i].astype(jnp.bfloat16)
 
             @pl.when(has_left)
             def _():
                 left_copy(kl).start()
 
-        kt = s - 2 - jnp.maximum(z, depth - 1 - z)
-
-        @pl.when(kt == 0)
+        kc = s - LAG * (1 + reach)
+
+        @pl.when(jnp.logical_and(inside(kc), z == root_of(kc)))
+        def _():
+            @pl.when(has_left)
+            def _():
+                toward_right(kc).wait_recv()
+                for i in range(per_b):
+                    at = 2 * per_a + i
+                    own[kc, at] = own[kc, at] + root_left[kc, i].astype(jnp.float32)
+
+            @pl.when(has_right)
+            def _():
+                toward_left(kc).wait_recv()
+                for i in range(per_b):
+                    at = 2 * per_a + i
+                    own[kc, at] = own[kc, at] + root_right[kc, i].astype(jnp.float32)
+
+            for i in range(per_b):
+                swap_out[kc, i] = own[kc, 2 * per_a + i].astype(jnp.bfloat16)
+            swap_copy(kc).start()
+
+        @pl.when(s == LAG * (2 + reach))
         def _():
             for j in range(1, group):
                 info_copy(j).wait_recv()
 
+        kw = s - LAG * (2 + reach)
+
+        @pl.when(jnp.logical_and(inside(kw), z == root_of(kw)))
+        def _():
+            swap_copy(kw).wait_recv()
+            for i in range(per_b):
+                total = own[kw, 2 * per_a + i] + swap_in[kw, i].astype(jnp.float32)
+                scaled(wide_mine + kw * per_b + i, total)
+
+            @pl.when(has_left)
+            def _():
+                spread_left(kw).start()
+
+            @pl.when(has_right)
+            def _():
+                spread_right(kw).start()
+
+            wide_copy(kw).start()
+
+        for d in range(1, reach + 1):
+            ko = s - LAG * (2 + reach + d)
+            gap = z - root_of(ko)
+
+            @pl.when(jnp.logical_and(inside(ko), gap == -d))
+            def _():
+                spread_left(ko).wait_recv()
+
+                @pl.when(has_left)
+                def _():
+                    spread_left(ko).start()
+
+                wide_copy(ko).start()
+
+            @pl.when(jnp.logical_and(inside(ko), gap == d))
+            def _():
+                spread_right(ko).wait_recv()
+
+                @pl.when(has_right)
+                def _():
+                    spread_right(ko).start()
+
+                wide_copy(ko).start()
+
+        kt = s - LAG * (2 + jnp.maximum(z, depth - 1 - z))
+
         @pl.when(inside(kt))
         def _():
             @pl.when(has_left)
             def _():
-                for i in range(CHUNK):
+                for i in range(per_a):
                     own[kt, i] = own[kt, i] + from_left[kt, i].astype(jnp.float32)
 
             @pl.when(has_right)
             def _():
-                for i in range(CHUNK):
+                for i in range(per_a):
                     own[kt, i] = own[kt, i] + from_right[kt, i].astype(jnp.float32)
 
-            for i in range(CHUNK):
-                v = q_mine * quarter + kt * CHUNK + i
-                row = info[v // rows_per, pl.ds(v % rows_per, 1), :]
-                scale = jnp.broadcast_to(row, (block, block)).T
-                weighted[v] = (scale * own[kt, i]).astype(jnp.bfloat16)
+            for i in range(per_a):
+                scaled(q_mine * column + kt * per_a + i, own[kt, i])
             wy_copy(kt).start()
             ws_copy(kt).start()
 
-        kd = kt - 1
+        kd = kt - LAG
 
         @pl.when(inside(kd))
         def _():
             wy_copy(kd).wait_recv()
             wf_copy(kd).start()
 
-        for n in range(2):
-            t = s * 2 + n
-
-            @pl.when(t < tiles)
-            def _():
-                flipped[t, :block, :] = plant[t, 0].T
-                flipped[t, block:, :] = plant[t, 1].T
+        @pl.when(s < tiles)
+        def _():
+            flipped[s, :block, :] = plant[s, 0].T
+            flipped[s, block:, :] = plant[s, 1].T
 
         return carry
 
-    steps = max(chunks + 3 + depth - 1, (tiles + 1) // 2)
+    steps = max(CHUNKS + LAG * max(depth + 2, 2 + 2 * reach), tiles)
     lax.fori_loop(0, steps, step, 0)
 
-    def arrived(k, carry):
-        ws_copy(k).wait_recv()
-        wf_copy(k).wait_recv()
-        return carry
-
-    lax.fori_loop(0, chunks, arrived, 0)
+    def whole_part(q):
+        return weighted.at[pl.ds(q * column, column)]
+
+    def whole_wide(first, amount):
+        return weighted.at[pl.ds(first, amount)]
+
+    def all_of(src, send, recv):
+        return copy(src, src, sends.at[send], ends_r.at[recv], sib)
+
+    all_of(whole_part(q_sib), 5, 0).wait_recv()
+    all_of(whole_part(q_diag), 6, 1).wait_recv()
+    all_of(whole_wide(wide_sib, square), 7, 2).wait_recv()
 
     for t in range(tiles):
         key = pair_key[t]
@@ -294,24 +438,50 @@
     for j in range(1, group):
         info_copy(j).wait_send()
 
-    def sent(k, carry):
-        sib_copy(k).wait_send()
-        y_copy(k).wait_send()
-        ws_copy(k).wait_send()
-        wy_copy(k).wait_send()
-        wf_copy(k).wait_send()
-
-        @pl.when(has_right)
-        def _():
-            right_copy(k).wait_send()
-
-        @pl.when(has_left)
-        def _():
-            left_copy(k).wait_send()
-
-        return carry
-
-    lax.fori_loop(0, chunks, sent, 0)
+    all_of(sib_out, 0, 0).wait_send()
+    all_of(y_out, 1, 0).wait_send()
+    all_of(whole_part(q_mine), 4, 0).wait_send()
+    all_of(whole_part(q_mine), 5, 0).wait_send()
+    all_of(whole_part(q_y), 6, 0).wait_send()
+    all_of(whole_wide(wide_mine, square), 7, 0).wait_send()
+
+    @pl.when(has_right)
+    def _():
+        all_of(right_out, 2, 0).wait_send()
+
+    @pl.when(has_left)
+    def _():
+        all_of(left_out, 3, 0).wait_send()
+
+    some = square // 2
+
+    @pl.when(z < reach - 1)
+    def _():
+        all_of(whole_wide(wide_mine, square), 8, 0).wait_send()
+
+    @pl.when(z == reach - 1)
+    def _():
+        all_of(whole_wide(wide_mine, some), 8, 0).wait_send()
+        all_of(whole_wide(wide_mine, some), 10, 0).wait_send()
+        all_of(whole_wide(wide_mine, some), 11, 0).wait_send()
+
+    @pl.when(z > reach)
+    def _():
+        all_of(whole_wide(wide_mine, square), 9, 0).wait_send()
+
+    @pl.when(z == reach)
+    def _():
+        all_of(whole_wide(wide_mine, some), 9, 0).wait_send()
+        all_of(whole_wide(wide_mine, some), 10, 0).wait_send()
+        all_of(whole_wide(wide_mine, some), 12, 0).wait_send()
+
+    @pl.when(jnp.logical_and(z >= reach, has_right))
+    def _():
+        all_of(whole_wide(wide_mine, square), 11, 0).wait_send()
+
+    @pl.when(jnp.logical_and(z < reach, has_left))
+    def _():
+        all_of(whole_wide(wide_mine, square), 12, 0).wait_send()
 
 
 def per_device(direction, plant, tile_pairs, mic_weight):
@@ -320,8 +490,8 @@
     tiles = plant.shape[0]
     bins = mic_weight.shape[0]
     group = SBLK // units
-    quarter = MBLK // 4
-    chunks = quarter // CHUNK
+    per_a = MBLK // 8 // CHUNKS
+    per_b = MBLK // 4 // CHUNKS
     rows_per = MBLK // group
 
     if bins == 1:
@@ -344,8 +514,9 @@
     vmem = pl.BlockSpec(memory_space=pltpu.VMEM)
     hbm = pl.BlockSpec(memory_space=pl.ANY)
     smem = pl.BlockSpec(memory_space=pltpu.SMEM)
-    piece = (chunks, CHUNK, block, width)
-    double = (chunks, 2 * CHUNK, block, width)
+    piece = (CHUNKS, per_a, block, width)
+    large = (CHUNKS, per_b, block, width)
+    mixed = (CHUNKS, 2 * per_a + per_b, block, width)
     return pl.pallas_call(
         functools.partial(kernel, group),
         out_shape=jax.ShapeDtypeStruct(direction.shape, f32),
@@ -359,19 +530,14 @@
             pltpu.VMEM((tiles * units + 1, block, width), f32),
             pltpu.VMEM((tiles, 2 * block, block), bf16),
             pltpu.VMEM((2 * block, units * width), bf16),
-            pltpu.VMEM(double, bf16),
-            pltpu.VMEM(double, bf16),
-            pltpu.VMEM(double, f32),
-            pltpu.VMEM(piece, bf16),
-            pltpu.VMEM(piece, bf16),
-            pltpu.VMEM(piece, bf16),
-            pltpu.VMEM(piece, bf16),
-            pltpu.VMEM(piece, bf16),
-            pltpu.VMEM(piece, bf16),
+            pltpu.VMEM(mixed, bf16),
+            pltpu.VMEM(mixed, bf16),
+            pltpu.VMEM(mixed, f32),
+        ] + [pltpu.VMEM(piece, bf16)] * 6 + [pltpu.VMEM(large, bf16)] * 5 + [
             pltpu.VMEM((MBLK + 1, block, width), bf16),
             pltpu.VMEM((tiles, block, units * width), bf16),
-            dma((3,)), dma((group,)), dma((group,)),
-        ] + [dma((chunks,)) for _ in range(14)],
+            dma((3,)), dma((group,)), dma((group,)), dma((13,)),
+        ] + [dma((CHUNKS,))] * 9 + [dma((3,))],
         compiler_params=pltpu.CompilerParams(
             collective_id=0, has_side_effects=True, vmem_limit_bytes=60 * 1024 * 1024
         ),

time: 84.6 us -> 69.5 us (0.82)
  Pallas kernels: 80.1 us -> 65 us
    pallas_call x1, Pallas kernels: 80.1 us -> 65 us  [per_device(): pl.pallas_call(functools.partial(kernel, group), out_shape=jax.ShapeDtype...]
where the time goes in v3:
time: 69.5 us; the launch traced here: 69.2 us
  Pallas kernels  65 us (94%)
  other arithmetic  2.7 us (4%)
  local copies, waits for them, and re-layouts  1.57 us (2%)
    pallas_call x1, Pallas kernels, per_device(): pl.pallas_call(functools.partial(kernel, group), out_shape=jax.ShapeDtype...  65 us
    unnamed x1, local copies, waits for them, and re-layouts  1.57 us

profile of v3, /device:TPU:1, one launch (start us, length us, event | category | flops | bytes accessed | tf_op | source)
XLA Modules:
  0.0 69.2 jit_solution(14308658607911664176)
XLA Ops:
  0.0 1.3 %fusion.pair_key = s32[26]{0:T(128)} fusion(s32[26,2]{0,1:T(2,128)} %param.6), kind=kLoop, calls=%fused_computation.8 | loop fusion | flops 338 | bytes 312 | tf_op jit(solution)/shard_map/add | solution.py:506
  1.3 0.8 %add_bitcast_fusion = (s32[26]{0:T(128)S(1)}, s32[26,1]{0,1:T(1,128)S(1)}) fusion(s32[26,2]{0,1:T(2,128)} %param.6), kind=kLoop, calls=%fused_computation.12 | loop fusion | flops 338 | bytes 416 | tf_op jit(solution)/shard_map/eq | solution.py:509
  2.0 0.1 select_reduce_fusion
  2.1 0.6 broadcast_subtract_fusion.fwd_idx
  2.7 65.0 %pressure_matching.1 = f32[2,128,128]{2,1,0:T(8,128)} custom-call(s32[256]{0:T(256)} %broadcast_subtract_fusion.fwd_idx, s32[26]{0:T(128)} %fusion.pair_key, f32[2,128,128]{2,1,0:T(8,128)} %direction_in.1, bf16[26,2,128,128]{3,2,1,0:T(8,128)(2,1)} %plant_in.1, f32[8,128]{1,0:T(8,128)} %bitcast.9), custom_call_target="tpu_custom_call" | custom-call | tf_op jit(solution)/shard_map/pressure_matching/pallas_call | solution.py:520
  67.7 1.6 %copy.6 = f32[2,128,128]{2,1,0:T(8,128)} copy(f32[2,128,128]{2,1,0:T(8,128)} %pressure_matching.1) | data formatting | bytes 262144
  (1 shorter events, 0.0 us)

commit v4 on v3

--- a/solution.py
+++ b/solution.py
@@ -19,11 +19,11 @@
 
 
 def kernel(
-    group, fwd_idx, pair_key, direction_in, plant_in, weights_in, out,
-    direction, plant, weights, info, products, flipped, fields, sib_out, sib_in, own,
+    group, pairs, direction_in, plant_in, weights_in, out,
+    direction, plant, weights, info, power, table, slots, products, flipped, fields, sib_out, sib_in, own,
     y_out, y_in, right_out, left_out, from_left, from_right,
     root_out, root_left, root_right, swap_out, swap_in, weighted, stacked,
-    load_s, info_s, info_r, sends,
+    load_s, info_s, info_r, power_s, power_r, sends,
     sib_r, y_r, right_r, left_r, wy_r, toward_right_r, toward_left_r, swap_r, spread_r, ends_r,
 ):
     units, block, width = direction.shape
@@ -75,6 +75,17 @@
     for j in range(1, group):
         pl.semaphore_signal(barrier, inc=1, device_id={"spk": peer(j)}, device_id_type=MESH)
 
+    row_id = lax.broadcasted_iota(jnp.int32, (8, MBLK), 0)
+    lane_id = lax.broadcasted_iota(jnp.int32, (8, MBLK), 1)
+    found = jnp.full((8, MBLK), tiles * units, jnp.int32)
+    for t in range(tiles):
+        u = pairs[0, t] % units
+        hit = jnp.logical_and(row_id == u, lane_id == pairs[1, t])
+        found = jnp.where(hit, t * units + u, found)
+    table[...] = found
+    to_slots = pltpu.make_async_copy(table, slots, load_s.at[3])
+    to_slots.start()
+
     loads[0].wait()
     lane = lax.broadcasted_iota(jnp.int32, (block, width), 1)
     for u in range(units):
@@ -85,25 +96,23 @@
         fields[block:, u * width:(u + 1) * width] = turned.astype(jnp.bfloat16)
     loads[1].wait()
 
-    def pack(t, power):
-        p0 = plant[t, 0]
-        p1 = plant[t, 1]
+    def multiply(t, carry):
         both = jnp.dot(
-            jnp.concatenate([p0, p1], axis=1), fields[...], preferred_element_type=jnp.float32
+            jnp.concatenate([plant[t, 0], plant[t, 1]], axis=1),
+            fields[...],
+            preferred_element_type=jnp.float32,
         )
         for u in range(units):
             products[t * units + u] = both[:, u * width:(u + 1) * width]
-        f0 = p0.astype(jnp.float32)
-        f1 = p1.astype(jnp.float32)
-        squares = f0 * f0 + f1 * f1
-        return power + jnp.sum(squares.reshape(block // 8, 8, block), axis=0)
-
-    power = lax.fori_loop(0, tiles, pack, jnp.zeros((8, block), jnp.float32))
+        return carry
+
+    lax.fori_loop(0, tiles, multiply, 0, unroll=2)
     products[tiles * units] = jnp.zeros((block, width), jnp.float32)
     weighted[MBLK] = jnp.zeros((block, width), jnp.bfloat16)
     loads[2].wait()
-    info[rank, :rows_per, :] = weights[...]
-    info[rank, rows_per:, :] = power
+    info[rank] = weights[...]
+    power[rank] = jnp.zeros((8, block), jnp.float32)
+    to_slots.wait()
 
     pl.semaphore_wait(barrier, group - 1)
 
@@ -116,6 +125,9 @@
     def wide(first, k):
         return weighted.at[pl.ds(first + k * per_b, per_b)]
 
+    def power_copy(j):
+        return copy(power.at[rank], power.at[rank], power_s.at[j], power_r.at[j], peer(j))
+
     def sib_copy(k):
         return copy(sib_out.at[k], sib_in.at[k], sends.at[0], sib_r.at[k], sib)
 
@@ -159,9 +171,9 @@
         info_copy(j).start()
 
     def product(v):
-        total = products[fwd_idx[v * units]]
+        total = products[slots[0, v]]
         for u in range(1, units):
-            total += products[fwd_idx[v * units + u]]
+            total += products[slots[u, v]]
         return total
 
     def inside(k):
@@ -174,6 +186,8 @@
 
     def root_of(k):
         return reach - 1 + k % 2
+
+    first = 6
 
     def step(s, carry):
         @pl.when(inside(s))
@@ -187,12 +201,6 @@
                 at = k * per_b + i
                 sib_out[k, 2 * per_a + i] = product(wide_sib + at).astype(jnp.bfloat16)
             sib_copy(k).start()
-            for i in range(per_a):
-                at = k * per_a + i
-                own[k, i] = product(q_mine * column + at)
-                own[k, per_a + i] = product(q_y * column + at)
-            for i in range(per_b):
-                own[k, 2 * per_a + i] = product(wide_mine + k * per_b + i)
 
         k1 = s - LAG
 
@@ -200,13 +208,17 @@
         def _():
             sib_copy(k1).wait_recv()
             for i in range(per_a):
-                total = own[k1, per_a + i] + sib_in[k1, per_a + i].astype(jnp.float32)
+                total = product(q_y * column + k1 * per_a + i)
+                total += sib_in[k1, per_a + i].astype(jnp.float32)
                 y_out[k1, i] = total.astype(jnp.bfloat16)
             y_copy(k1).start()
+            for i in range(per_b):
+                at = per_a + i
+                total = product(wide_mine + k1 * per_b + i)
+                own[k1, at] = total + sib_in[k1, per_a + at].astype(jnp.float32)
             for i in range(per_a):
-                own[k1, i] = own[k1, i] + sib_in[k1, i].astype(jnp.float32)
-            for i in range(2 * per_a, 2 * per_a + per_b):
-                own[k1, i] = own[k1, i] + sib_in[k1, i].astype(jnp.float32)
+                total = product(q_mine * column + k1 * per_a + i)
+                own[k1, i] = total + sib_in[k1, i].astype(jnp.float32)
 
         for d in range(reach, 0, -1):
             kb = s - LAG * (1 + reach - d)
@@ -218,13 +230,13 @@
                 def _():
                     toward_right(kb).wait_recv()
                     for i in range(per_b):
-                        total = own[kb, 2 * per_a + i] + root_left[kb, i].astype(jnp.float32)
+                        total = own[kb, per_a + i] + root_left[kb, i].astype(jnp.float32)
                         root_out[kb, i] = total.astype(jnp.bfloat16)
 
                 @pl.when(jnp.logical_not(has_left))
                 def _():
                     for i in range(per_b):
-                        root_out[kb, i] = own[kb, 2 * per_a + i].astype(jnp.bfloat16)
+                        root_out[kb, i] = own[kb, per_a + i].astype(jnp.bfloat16)
 
                 toward_right(kb).start()
 
@@ -234,13 +246,13 @@
                 def _():
                     toward_left(kb).wait_recv()
                     for i in range(per_b):
-                        total = own[kb, 2 * per_a + i] + root_right[kb, i].astype(jnp.float32)
+                        total = own[kb, per_a + i] + root_right[kb, i].astype(jnp.float32)
                         root_out[kb, i] = total.astype(jnp.bfloat16)
 
                 @pl.when(jnp.logical_not(has_right))
                 def _():
                     for i in range(per_b):
-                        root_out[kb, i] = own[kb, 2 * per_a + i].astype(jnp.bfloat16)
+                        root_out[kb, i] = own[kb, per_a + i].astype(jnp.bfloat16)
 
                 toward_left(kb).start()
 
@@ -306,18 +318,18 @@
             def _():
                 toward_right(kc).wait_recv()
                 for i in range(per_b):
-                    at = 2 * per_a + i
+                    at = per_a + i
                     own[kc, at] = own[kc, at] + root_left[kc, i].astype(jnp.float32)
 
             @pl.when(has_right)
             def _():
                 toward_left(kc).wait_recv()
                 for i in range(per_b):
-                    at = 2 * per_a + i
+                    at = per_a + i
                     own[kc, at] = own[kc, at] + root_right[kc, i].astype(jnp.float32)
 
             for i in range(per_b):
-                swap_out[kc, i] = own[kc, 2 * per_a + i].astype(jnp.bfloat16)
+                swap_out[kc, i] = own[kc, per_a + i].astype(jnp.bfloat16)
             swap_copy(kc).start()
 
         @pl.when(s == LAG * (2 + reach))
@@ -331,7 +343,7 @@
         def _():
             swap_copy(kw).wait_recv()
             for i in range(per_b):
-                total = own[kw, 2 * per_a + i] + swap_in[kw, i].astype(jnp.float32)
+                total = own[kw, per_a + i] + swap_in[kw, i].astype(jnp.float32)
                 scaled(wide_mine + kw * per_b + i, total)
 
             @pl.when(has_left)
@@ -394,14 +406,30 @@
             wy_copy(kd).wait_recv()
             wf_copy(kd).start()
 
-        @pl.when(s < tiles)
-        def _():
-            flipped[s, :block, :] = plant[s, 0].T
-            flipped[s, block:, :] = plant[s, 1].T
+        n = s - first
+
+        @pl.when(jnp.logical_and(n >= 0, n < tiles // 2))
+        def _():
+            squares = power[rank]
+            for m in range(2):
+                p0 = plant[2 * n + m, 0]
+                p1 = plant[2 * n + m, 1]
+                flipped[n, :block, m * block:(m + 1) * block] = p0.T
+                flipped[n, block:, m * block:(m + 1) * block] = p1.T
+                f0 = p0.astype(jnp.float32)
+                f1 = p1.astype(jnp.float32)
+                both = f0 * f0 + f1 * f1
+                squares += jnp.sum(both.reshape(block // 8, 8, block), axis=0)
+            power[rank] = squares
+
+        @pl.when(n == tiles // 2)
+        def _():
+            for j in range(1, group):
+                power_copy(j).start()
 
         return carry
 
-    steps = max(CHUNKS + LAG * max(depth + 2, 2 + 2 * reach), tiles)
+    steps = max(CHUNKS + LAG * max(depth + 2, 2 + 2 * reach), first + tiles // 2 + 1)
     lax.fori_loop(0, steps, step, 0)
 
     def whole_part(q):
@@ -418,15 +446,18 @@
     all_of(whole_wide(wide_sib, square), 7, 2).wait_recv()
 
     for t in range(tiles):
-        key = pair_key[t]
+        unit = pairs[0, t] % units
+        rows = slice((t % 2) * block, (t % 2 + 1) * block)
         for u in range(units):
-            at = jnp.where(key % units == u, key // units, MBLK)
-            stacked[t, :, u * width:(u + 1) * width] = weighted[at]
+            at = jnp.where(unit == u, pairs[1, t], MBLK)
+            stacked[t // 2, rows, u * width:(u + 1) * width] = weighted[at]
     total = jnp.zeros((2 * block, units * width), jnp.float32)
-    for t in range(tiles):
-        total += jnp.dot(flipped[t], stacked[t], preferred_element_type=jnp.float32)
-
-    power_sum = jnp.sum(info[:, rows_per:, :], axis=0)
+    for n in range(tiles // 2):
+        total += jnp.dot(flipped[n], stacked[n], preferred_element_type=jnp.float32)
+
+    for j in range(1, group):
+        power_copy(j).wait_recv()
+    power_sum = jnp.sum(power[...], axis=0)
     power_sum = jnp.sum(jnp.sum(power_sum, axis=1, keepdims=True), axis=0, keepdims=True)
     coefficient = reg_weight * power_sum / SPEAKERS
     for u in range(units):
@@ -437,6 +468,7 @@
 
     for j in range(1, group):
         info_copy(j).wait_send()
+        power_copy(j).wait_send()
 
     all_of(sib_out, 0, 0).wait_send()
     all_of(y_out, 1, 0).wait_send()
@@ -501,13 +533,6 @@
         weights = lax.dynamic_slice(
             whole, (device_id // group, (device_id % group) * rows_per, 0), (1, rows_per, block)
         )[0]
-
-    unit = tile_pairs[:, 0] % units
-    pair_key = tile_pairs[:, 1] * units + unit
-    last = tiles * units
-    slot = jnp.arange(tiles, dtype=jnp.int32) * units + unit
-    hit = pair_key[:, None] == jnp.arange(MBLK * units, dtype=jnp.int32)[None, :]
-    fwd_idx = last - jnp.sum(jnp.where(hit, (last - slot)[:, None], 0), axis=0)
 
     bf16, f32 = jnp.bfloat16, jnp.float32
     dma = pltpu.SemaphoreType.DMA
@@ -520,29 +545,32 @@
     return pl.pallas_call(
         functools.partial(kernel, group),
         out_shape=jax.ShapeDtypeStruct(direction.shape, f32),
-        in_specs=[smem, smem, hbm, hbm, hbm],
+        in_specs=[smem, hbm, hbm, hbm],
         out_specs=vmem,
         scratch_shapes=[
             pltpu.VMEM(direction.shape, f32),
             pltpu.VMEM(plant.shape, bf16),
             pltpu.VMEM(weights.shape, f32),
-            pltpu.VMEM((group, rows_per + 8, block), f32),
+            pltpu.VMEM((group, rows_per, block), f32),
+            pltpu.VMEM((group, 8, block), f32),
+            pltpu.VMEM((8, MBLK), jnp.int32),
+            pltpu.SMEM((8, MBLK), jnp.int32),
             pltpu.VMEM((tiles * units + 1, block, width), f32),
-            pltpu.VMEM((tiles, 2 * block, block), bf16),
+            pltpu.VMEM((tiles // 2, 2 * block, 2 * block), bf16),
             pltpu.VMEM((2 * block, units * width), bf16),
             pltpu.VMEM(mixed, bf16),
             pltpu.VMEM(mixed, bf16),
-            pltpu.VMEM(mixed, f32),
+            pltpu.VMEM((CHUNKS, per_a + per_b, block, width), f32),
         ] + [pltpu.VMEM(piece, bf16)] * 6 + [pltpu.VMEM(large, bf16)] * 5 + [
             pltpu.VMEM((MBLK + 1, block, width), bf16),
-            pltpu.VMEM((tiles, block, units * width), bf16),
-            dma((3,)), dma((group,)), dma((group,)), dma((13,)),
+            pltpu.VMEM((tiles // 2, 2 * block, units * width), bf16),
+            dma((4,)), dma((group,)), dma((group,)), dma((group,)), dma((group,)), dma((13,)),
         ] + [dma((CHUNKS,))] * 9 + [dma((3,))],
         compiler_params=pltpu.CompilerParams(
             collective_id=0, has_side_effects=True, vmem_limit_bytes=60 * 1024 * 1024
         ),
         name="pressure_matching",
-    )(fwd_idx, pair_key, direction, plant, weights)
+    )(tile_pairs.T, direction, plant, weights)
 
 
 def solution(mesh):

time: 69.5 us -> 65.5 us (0.942)
  other arithmetic: 2.7 us -> 0 us
  Pallas kernels: 65 us -> 63.8 us
    add x1 -> x0, other arithmetic: 1.27 us -> none  [per_device(): pair_key = tile_pairs[:, 1] * units + unit]
    pallas_call x1, Pallas kernels: 65 us -> 63.8 us  [per_device(): pl.pallas_call(functools.partial(kernel, group), out_shape=jax.ShapeDtype...]
    eq x1 -> x0, other arithmetic: 0.76 us -> none  [per_device(): pair_key[:, None] == jnp.arange(MBLK * units, dtype=jnp.int32)[None, :]]
where the time goes in v4:
time: 65.5 us; the launch traced here: 65.4 us
  Pallas kernels  63.8 us (97%)
  local copies, waits for them, and re-layouts  1.57 us (2%)
    pallas_call x1, Pallas kernels, per_device(): pl.pallas_call(functools.partial(kernel, group), out_shape=jax.ShapeDtype...  63.8 us
    unnamed x1, local copies, waits for them, and re-layouts  1.57 us

profile of v4, /device:TPU:1, one launch (start us, length us, event | category | flops | bytes accessed | tf_op | source)
XLA Modules:
  0.0 65.4 jit_solution(9878822205847228917)
XLA Ops:
  0.0 63.8 %pressure_matching.1 = f32[2,128,128]{2,1,0:T(8,128)} custom-call(s32[2,26]{1,0:T(2,128)} %bitcast.3, f32[2,128,128]{2,1,0:T(8,128)} %direction_in.1, bf16[26,2,128,128]{3,2,1,0:T(8,128)(2,1)} %plant_in.1, f32[8,128]{1,0:T(8,128)} %bitcast.2), custom_call_target="tpu_custom_call" | custom-call | tf_op jit(solution)/shard_map/pressure_matching/pallas_call | solution.py:545
  63.8 1.6 %copy.6 = f32[2,128,128]{2,1,0:T(8,128)} copy(f32[2,128,128]{2,1,0:T(8,128)} %pressure_matching.1) | data formatting | bytes 262144

commit v5 on v4

--- a/solution.py
+++ b/solution.py
@@ -63,10 +63,16 @@
             device_id={"spk": device}, device_id_type=MESH,
         )
 
+    early = tiles // 4
     loads = [
         pltpu.make_async_copy(src, dst, load_s.at[n])
         for n, (src, dst) in enumerate(
-            [(direction_in, direction), (plant_in, plant), (weights_in, weights)]
+            [
+                (direction_in, direction),
+                (plant_in.at[pl.ds(0, early)], plant.at[pl.ds(0, early)]),
+                (plant_in.at[pl.ds(early, tiles - early)], plant.at[pl.ds(early, tiles - early)]),
+                (weights_in, weights),
+            ]
         )
     ]
     for load in loads:
@@ -83,7 +89,7 @@
         hit = jnp.logical_and(row_id == u, lane_id == pairs[1, t])
         found = jnp.where(hit, t * units + u, found)
     table[...] = found
-    to_slots = pltpu.make_async_copy(table, slots, load_s.at[3])
+    to_slots = pltpu.make_async_copy(table, slots, load_s.at[4])
     to_slots.start()
 
     loads[0].wait()
@@ -106,10 +112,12 @@
             products[t * units + u] = both[:, u * width:(u + 1) * width]
         return carry
 
-    lax.fori_loop(0, tiles, multiply, 0, unroll=2)
+    lax.fori_loop(0, early, multiply, 0, unroll=2)
+    loads[2].wait()
+    lax.fori_loop(early, tiles, multiply, 0, unroll=4)
     products[tiles * units] = jnp.zeros((block, width), jnp.float32)
     weighted[MBLK] = jnp.zeros((block, width), jnp.bfloat16)
-    loads[2].wait()
+    loads[3].wait()
     info[rank] = weights[...]
     power[rank] = jnp.zeros((8, block), jnp.float32)
     to_slots.wait()
@@ -187,7 +195,10 @@
     def root_of(k):
         return reach - 1 + k % 2
 
-    first = 6
+    first = 10
+
+    def after(hops):
+        return 1 + LAG * (hops - 1)
 
     def step(s, carry):
         @pl.when(inside(s))
@@ -202,7 +213,7 @@
                 sib_out[k, 2 * per_a + i] = product(wide_sib + at).astype(jnp.bfloat16)
             sib_copy(k).start()
 
-        k1 = s - LAG
+        k1 = s - after(1)
 
         @pl.when(inside(k1))
         def _():
@@ -221,7 +232,7 @@
                 own[k1, i] = total + sib_in[k1, i].astype(jnp.float32)
 
         for d in range(reach, 0, -1):
-            kb = s - LAG * (1 + reach - d)
+            kb = s - after(1 + reach - d)
             gap = z - root_of(kb)
 
             @pl.when(jnp.logical_and(inside(kb), gap == -d))
@@ -256,7 +267,7 @@
 
                 toward_left(kb).start()
 
-        k2 = s - 2 * LAG
+        k2 = s - after(2)
 
         @pl.when(inside(k2))
         def _():
@@ -264,7 +275,7 @@
             for i in range(per_a):
                 own[k2, i] = own[k2, i] + y_in[k2, i].astype(jnp.float32)
 
-        kr = s - LAG * (2 + z)
+        kr = s - after(2 + z)
 
         @pl.when(inside(kr))
         def _():
@@ -287,7 +298,7 @@
             def _():
                 right_copy(kr).start()
 
-        kl = s - LAG * (2 + depth - 1 - z)
+        kl = s - after(2 + depth - 1 - z)
 
         @pl.when(inside(kl))
         def _():
@@ -310,7 +321,7 @@
             def _():
                 left_copy(kl).start()
 
-        kc = s - LAG * (1 + reach)
+        kc = s - after(1 + reach)
 
         @pl.when(jnp.logical_and(inside(kc), z == root_of(kc)))
         def _():
@@ -332,12 +343,12 @@
                 swap_out[kc, i] = own[kc, per_a + i].astype(jnp.bfloat16)
             swap_copy(kc).start()
 
-        @pl.when(s == LAG * (2 + reach))
+        @pl.when(s == after(2 + reach))
         def _():
             for j in range(1, group):
                 info_copy(j).wait_recv()
 
-        kw = s - LAG * (2 + reach)
+        kw = s - after(2 + reach)
 
         @pl.when(jnp.logical_and(inside(kw), z == root_of(kw)))
         def _():
@@ -357,7 +368,7 @@
             wide_copy(kw).start()
 
         for d in range(1, reach + 1):
-            ko = s - LAG * (2 + reach + d)
+            ko = s - after(2 + reach + d)
             gap = z - root_of(ko)
 
             @pl.when(jnp.logical_and(inside(ko), gap == -d))
@@ -380,7 +391,7 @@
 
                 wide_copy(ko).start()
 
-        kt = s - LAG * (2 + jnp.maximum(z, depth - 1 - z))
+        kt = s - after(2 + jnp.maximum(z, depth - 1 - z))
 
         @pl.when(inside(kt))
         def _():
@@ -429,7 +440,7 @@
 
         return carry
 
-    steps = max(CHUNKS + LAG * max(depth + 2, 2 + 2 * reach), first + tiles // 2 + 1)
+    steps = max(CHUNKS + after(max(depth + 2, 2 + 2 * reach)), first + tiles // 2 + 1)
     lax.fori_loop(0, steps, step, 0)
 
     def whole_part(q):
@@ -564,7 +575,7 @@
         ] + [pltpu.VMEM(piece, bf16)] * 6 + [pltpu.VMEM(large, bf16)] * 5 + [
             pltpu.VMEM((MBLK + 1, block, width), bf16),
             pltpu.VMEM((tiles // 2, 2 * block, units * width), bf16),
-            dma((4,)), dma((group,)), dma((group,)), dma((group,)), dma((group,)), dma((13,)),
+            dma((5,)), dma((group,)), dma((group,)), dma((group,)), dma((group,)), dma((13,)),
         ] + [dma((CHUNKS,))] * 9 + [dma((3,))],
         compiler_params=pltpu.CompilerParams(
             collective_id=0, has_side_effects=True, vmem_limit_bytes=60 * 1024 * 1024

time: 65.5 us -> 64.2 us (0.980)
  Pallas kernels: 63.8 us -> 62.5 us
    pallas_call x1, Pallas kernels: 63.8 us -> 62.5 us  [per_device(): pl.pallas_call(functools.partial(kernel, group), out_shape=jax.ShapeDtype...]
where the time goes in v5:
time: 64.2 us; the launch traced here: 64.1 us
  Pallas kernels  62.5 us (97%)
  local copies, waits for them, and re-layouts  1.57 us (2%)
    pallas_call x1, Pallas kernels, per_device(): pl.pallas_call(functools.partial(kernel, group), out_shape=jax.ShapeDtype...  62.5 us
    unnamed x1, local copies, waits for them, and re-layouts  1.57 us

profile of v5, /device:TPU:1, one launch (start us, length us, event | category | flops | bytes accessed | tf_op | source)
XLA Modules:
  0.0 64.1 jit_solution(3144737326116798272)
XLA Ops:
  0.0 62.5 %pressure_matching.1 = f32[2,128,128]{2,1,0:T(8,128)} custom-call(s32[2,26]{1,0:T(2,128)} %bitcast.3, f32[2,128,128]{2,1,0:T(8,128)} %direction_in.1, bf16[26,2,128,128]{3,2,1,0:T(8,128)(2,1)} %plant_in.1, f32[8,128]{1,0:T(8,128)} %bitcast.2), custom_call_target="tpu_custom_call" | custom-call | tf_op jit(solution)/shard_map/pressure_matching/pallas_call | solution.py:556
  62.5 1.6 %copy.6 = f32[2,128,128]{2,1,0:T(8,128)} copy(f32[2,128,128]{2,1,0:T(8,128)} %pressure_matching.1) | data formatting | bytes 262144

commit v6 on v5

--- a/solution.py
+++ b/solution.py
@@ -11,7 +11,7 @@
 MBLK = 128
 SPEAKERS = 4096
 CHUNKS = 16
-LAG = 2
+LAG = 3
 
 reg_weight = 0.25
 
@@ -195,7 +195,7 @@
     def root_of(k):
         return reach - 1 + k % 2
 
-    first = 10
+    first = 12
 
     def after(hops):
         return 1 + LAG * (hops - 1)

time: 64.2 us -> 66.4 us (1.034)
  Pallas kernels: 62.5 us -> 64.6 us
    pallas_call x1, Pallas kernels: 62.5 us -> 64.6 us  [per_device(): pl.pallas_call(functools.partial(kernel, group), out_shape=jax.ShapeDtype...]
where the time goes in v6:
time: 66.4 us; the launch traced here: 66.2 us
  Pallas kernels  64.6 us (97%)
  local copies, waits for them, and re-layouts  1.57 us (2%)
    pallas_call x1, Pallas kernels, per_device(): pl.pallas_call(functools.partial(kernel, group), out_shape=jax.ShapeDtype...  64.6 us
    unnamed x1, local copies, waits for them, and re-layouts  1.57 us

profile of v6, /device:TPU:1, one launch (start us, length us, event | category | flops | bytes accessed | tf_op | source)
XLA Modules:
  0.0 66.2 jit_solution(15560403010103500466)
XLA Ops:
  0.0 64.6 %pressure_matching.1 = f32[2,128,128]{2,1,0:T(8,128)} custom-call(s32[2,26]{1,0:T(2,128)} %bitcast.3, f32[2,128,128]{2,1,0:T(8,128)} %direction_in.1, bf16[26,2,128,128]{3,2,1,0:T(8,128)(2,1)} %plant_in.1, f32[8,128]{1,0:T(8,128)} %bitcast.2), custom_call_target="tpu_custom_call" | custom-call | tf_op jit(solution)/shard_map/pressure_matching/pallas_call | solution.py:556
  64.7 1.6 %copy.6 = f32[2,128,128]{2,1,0:T(8,128)} copy(f32[2,128,128]{2,1,0:T(8,128)} %pressure_matching.1) | data formatting | bytes 262144

commit v7 on v5

--- a/solution.py
+++ b/solution.py
@@ -22,7 +22,7 @@
     group, pairs, direction_in, plant_in, weights_in, out,
     direction, plant, weights, info, power, table, slots, products, flipped, fields, sib_out, sib_in, own,
     y_out, y_in, right_out, left_out, from_left, from_right,
-    root_out, root_left, root_right, swap_out, swap_in, weighted, stacked,
+    root_out, root_left, root_right, swap_out, swap_in, weighted,
     load_s, info_s, info_r, power_s, power_r, sends,
     sib_r, y_r, right_r, left_r, wy_r, toward_right_r, toward_left_r, swap_r, spread_r, ends_r,
 ):
@@ -102,7 +102,7 @@
         fields[block:, u * width:(u + 1) * width] = turned.astype(jnp.bfloat16)
     loads[1].wait()
 
-    def multiply(t, carry):
+    def multiply(t):
         both = jnp.dot(
             jnp.concatenate([plant[t, 0], plant[t, 1]], axis=1),
             fields[...],
@@ -110,11 +110,11 @@
         )
         for u in range(units):
             products[t * units + u] = both[:, u * width:(u + 1) * width]
-        return carry
-
-    lax.fori_loop(0, early, multiply, 0, unroll=2)
-    loads[2].wait()
-    lax.fori_loop(early, tiles, multiply, 0, unroll=4)
+
+    for t in range(tiles):
+        if t == early:
+            loads[2].wait()
+        multiply(t)
     products[tiles * units] = jnp.zeros((block, width), jnp.float32)
     weighted[MBLK] = jnp.zeros((block, width), jnp.bfloat16)
     loads[3].wait()
@@ -456,15 +456,16 @@
     all_of(whole_part(q_diag), 6, 1).wait_recv()
     all_of(whole_wide(wide_sib, square), 7, 2).wait_recv()
 
-    for t in range(tiles):
+    def fields_of(t):
         unit = pairs[0, t] % units
-        rows = slice((t % 2) * block, (t % 2 + 1) * block)
-        for u in range(units):
-            at = jnp.where(unit == u, pairs[1, t], MBLK)
-            stacked[t // 2, rows, u * width:(u + 1) * width] = weighted[at]
+        return jnp.concatenate(
+            [weighted[jnp.where(unit == u, pairs[1, t], MBLK)] for u in range(units)], axis=1
+        )
+
     total = jnp.zeros((2 * block, units * width), jnp.float32)
     for n in range(tiles // 2):
-        total += jnp.dot(flipped[n], stacked[n], preferred_element_type=jnp.float32)
+        stacked = jnp.concatenate([fields_of(2 * n), fields_of(2 * n + 1)], axis=0)
+        total += jnp.dot(flipped[n], stacked, preferred_element_type=jnp.float32)
 
     for j in range(1, group):
         power_copy(j).wait_recv()
@@ -574,7 +575,6 @@
             pltpu.VMEM((CHUNKS, per_a + per_b, block, width), f32),
         ] + [pltpu.VMEM(piece, bf16)] * 6 + [pltpu.VMEM(large, bf16)] * 5 + [
             pltpu.VMEM((MBLK + 1, block, width), bf16),
-            pltpu.VMEM((tiles // 2, 2 * block, units * width), bf16),
             dma((5,)), dma((group,)), dma((group,)), dma((group,)), dma((group,)), dma((13,)),
         ] + [dma((CHUNKS,))] * 9 + [dma((3,))],
         compiler_params=pltpu.CompilerParams(

time: 64.2 us -> 64 us (level)
  no operation moved by 1% of the time
where the time goes in v7:
time: 64 us; the launch traced here: 63.8 us
  Pallas kernels  62.2 us (97%)
  local copies, waits for them, and re-layouts  1.57 us (2%)
    pallas_call x1, Pallas kernels, per_device(): pl.pallas_call(functools.partial(kernel, group), out_shape=jax.ShapeDtype...  62.2 us
    unnamed x1, local copies, waits for them, and re-layouts  1.57 us

profile of v7, /device:TPU:1, one launch (start us, length us, event | category | flops | bytes accessed | tf_op | source)
XLA Modules:
  0.0 63.8 jit_solution(13940053868988833813)
XLA Ops:
  0.0 62.2 %pressure_matching.1 = f32[2,128,128]{2,1,0:T(8,128)} custom-call(s32[2,26]{1,0:T(2,128)} %bitcast.3, f32[2,128,128]{2,1,0:T(8,128)} %direction_in.1, bf16[26,2,128,128]{3,2,1,0:T(8,128)(2,1)} %plant_in.1, f32[8,128]{1,0:T(8,128)} %bitcast.2), custom_call_target="tpu_custom_call" | custom-call | tf_op jit(solution)/shard_map/pressure_matching/pallas_call | solution.py:557
  62.2 1.6 %copy.6 = f32[2,128,128]{2,1,0:T(8,128)} copy(f32[2,128,128]{2,1,0:T(8,128)} %pressure_matching.1) | data formatting | bytes 262144
